TPU v7x, 128 devices: a whole 4x4x4 slice. The times are simulated.
128 devices in a mesh: group: 16 (over x, y), span: 8 (over z, core).
Axes of the slice: x: 4, y: 4, z: 4, core: 2. Of those that a mesh axis runs over, the one named last changes fastest.
Arguments:
- embeddings: float32 [49152, 1024], P(('group', 'span')), may hold values from -100 to 100
- cluster_ids: int32 [49152, 1], P(('group', 'span')), may hold values from 0 to 47; in each aligned block of 384 rows (0 to 383, 384 to 767, ...) at most 24 rows name the same one
- order: int32 [49152], P(('group', 'span')), may hold values from 0 to 49151, each once
Outputs:
- nearest: float32 [49152], P(('group', 'span'))
Inputs may be any that keep to these rules, and one draw needn't show every extreme that they name: `cluster_ids`: in the rows of one device no cluster appears more than 24 times, and some cluster appears exactly 24 times. `order`: each number appears once.
All inputs are finite; a program needn't handle non-finite values.
Results may differ from a plain program's by a relative error of at most 0.00048.
Values may be sent and summed in bfloat16 or wider, within the bound.
No kernel may reach another device: no remote copies, remote signals or barrier semaphores. Data moves between devices by JAX's collectives and lax.ppermute only.
A program may use at most 128 MiB of HBM per device.

v0:
```python
import jax
import jax.numpy as jnp
from jax import lax
from jax.sharding import PartitionSpec as P

CLUSTERS = 48
MOST = 24


def improve(best_score, query_units, query_cluster, query_order, key_units, key_cluster, key_order):
    scores = lax.dot_general(
        query_units, key_units, (((1,), (1,)), ((), ())), preferred_element_type=jnp.float32
    )
    allowed = (
        (query_cluster[:, None] == key_cluster[None, :])
        & (key_order[None, :] < query_order[:, None])
        & (query_cluster[:, None] >= 0)
    )
    return jnp.maximum(best_score, jnp.max(jnp.where(allowed, scores, jnp.float32(-1.0)), axis=1))


def per_device(embeddings, cluster_ids, order):
    row_count = embeddings.shape[0]
    width = embeddings.shape[1]
    group_size = lax.axis_size("group")
    unit = (
        embeddings * lax.rsqrt(jnp.sum(embeddings * embeddings, axis=1, keepdims=True) + 1e-06)
    ).astype(jnp.bfloat16)
    cluster = cluster_ids[:, 0]
    per_group = CLUSTERS // group_size
    capacity = per_group * MOST
    total_slots = group_size * capacity
    one_hot = (cluster[:, None] == jnp.arange(CLUSTERS, dtype=jnp.int32)[None, :]).astype(
        jnp.float32
    )
    positions = jnp.arange(row_count, dtype=jnp.int32)
    earlier = (positions[:, None] > positions[None, :]).astype(jnp.float32)
    prior_counts = jnp.dot(earlier, one_hot, preferred_element_type=jnp.float32)
    ranking = jnp.sum(prior_counts * one_hot, axis=1).astype(jnp.int32)
    owner = cluster // per_group
    slot_index = owner * capacity + cluster % per_group * MOST + ranking
    send_units = (
        jnp.zeros((total_slots, width), jnp.bfloat16)
        .at[slot_index]
        .set(unit)
        .reshape(group_size, capacity, width)
    )
    send_cluster = (
        jnp.full((total_slots,), -1, jnp.int32)
        .at[slot_index]
        .set(cluster)
        .reshape(group_size, capacity)
    )
    send_order = (
        jnp.zeros((total_slots,), jnp.int32).at[slot_index].set(order).reshape(group_size, capacity)
    )
    got_units, got_cluster, got_order = (
        lax.all_to_all(send_units, "group", split_axis=0, concat_axis=0, tiled=True),
        lax.all_to_all(send_cluster, "group", split_axis=0, concat_axis=0, tiled=True),
        lax.all_to_all(send_order, "group", split_axis=0, concat_axis=0, tiled=True),
    )
    query_units = got_units.reshape(total_slots, width)
    query_cluster = got_cluster.reshape(total_slots)
    query_order = got_order.reshape(total_slots)
    initial = jnp.full((total_slots,), -1.0, jnp.float32)
    best_score = improve(
        initial,
        query_units,
        query_cluster,
        query_order,
        lax.all_gather(query_units, "span", axis=0, tiled=True),
        lax.all_gather(query_cluster, "span", axis=0, tiled=True),
        lax.all_gather(query_order, "span", axis=0, tiled=True),
    )
    returned = lax.all_to_all(
        best_score.reshape(group_size, capacity), "group", split_axis=0, concat_axis=0, tiled=True
    )
    return returned.reshape(total_slots)[slot_index]


def solution(mesh):
    return jax.shard_map(
        per_device,
        mesh=mesh,
        in_specs=(P(("group", "span"), None), P(("group", "span"), None), P(("group", "span"))),
        out_specs=P(("group", "span")),
        check_vma=False,
    )
```

profile of v0, /device:TPU:1, one launch (start us, length us, event | category | flops | bytes accessed | tf_op | source)
XLA Modules:
  0.0 201.0 jit_solution(5479048095442846776)
XLA Ops:
  6.5 0.0 all-gather.4.cloned.1.call-start
  6.5 0.7 reduce
  7.2 0.2 fusion.3
  7.5 0.7 fusion.10
  8.2 1.6 multiply_reduce_fusion
  9.8 3.8 %scatter_custom_fusion.2 = bf16[1152,1024]{1,0:T(8,128)(2,1)S(1)} fusion(s32[384]{0:T(512)S(1)} %fusion.10, bf16[]{:T(256)} %constant.38.clone.1, f32[384,1024]{1,0:T(8,128)} %param.3, f32[384]{0:T(512)S(1)} %add_rsqrt_fusion), kind=kCustom, calls=%fused_computation.8 | custom fusion | flops 786432 | bytes 3934210 | tf_op jit(solution)/shard_map/scatter | solution.py:45
  13.6 37.2 %all_to_all.29 = bf16[16,72,1024]{2,1,0:T(8,128)(2,1)} all-to-all(bf16[16,72,1024]{2,1,0:T(8,128)(2,1)S(1)} %bitcast.10), channel_id=1, replica_groups=mesh['group'=16,'span'=8] {'group'}, dimensions={0} | all-to-all | bytes 4718592 | tf_op jit(solution)/shard_map/all_to_all | solution.py:58
  50.8 0.0 copy-start
  50.8 0.0 all-gather.4.cloned.1.call-update
  50.8 2.9 %scatter_custom_fusion = s32[1152]{0:T(1024)S(1)} fusion(s32[384]{0:T(512)S(1)} %fusion.10, s32[384]{0:T(512)S(1)} %reduce, s32[]{:T(128)} %constant.12.clone.1), kind=kCustom, calls=%fused_computation.24 | custom fusion | bytes 4612 | tf_op jit(solution)/shard_map/scatter | solution.py:51
  53.7 0.7 all_to_all.19
  54.4 4.1 %all-to-all-start = ((s32[16,1,72]{2,1,0:T(1,128)}), s32[16,1,72]{2,1,0:T(1,128)S(1)}, u32[]{:S(2)}, u32[]{:S(2)}) async-start(s32[16,1,72]{2,1,0:T(1,128)} %all_to_all.19), calls=%async_computation | async-start | bytes 16384 | tf_op jit(solution)/shard_map/all_to_all | solution.py:59
  58.5 3.1 %scatter_custom_fusion.1 = s32[1152]{0:T(1024)S(1)} fusion(s32[384]{0:T(512)S(1)} %fusion.10, s32[384]{0:T(512)} %param.5, s32[]{:T(128)} %constant.15.clone.1), kind=kCustom, calls=%fused_computation.22 | custom fusion | bytes 5120 | tf_op jit(solution)/shard_map/scatter | solution.py:55
  61.6 0.7 all_to_all.21
  62.3 2.6 %all-to-all-done = s32[16,1,72]{2,1,0:T(1,128)S(1)} async-done(((s32[16,1,72]{2,1,0:T(1,128)}), s32[16,1,72]{2,1,0:T(1,128)S(1)}, u32[]{:S(2)}, u32[]{:S(2)}) %all-to-all-start) | async-done | bytes 4640 | tf_op jit(solution)/shard_map/all_to_all | solution.py:59
  64.9 4.0 %all-to-all-start.1 = ((s32[16,1,72]{2,1,0:T(1,128)}), s32[16,1,72]{2,1,0:T(1,128)S(1)}, u32[]{:S(2)}, u32[]{:S(2)}) async-start(s32[16,1,72]{2,1,0:T(1,128)} %all_to_all.21), calls=%async_computation.1 | async-start | bytes 16384 | tf_op jit(solution)/shard_map/all_to_all | solution.py:60
  69.0 0.5 broadcast.68
  69.5 0.7 reduce.16
  70.1 0.1 eq.36
  70.2 5.1 %all-to-all-done.1 = s32[16,1,72]{2,1,0:T(1,128)S(1)} async-done(((s32[16,1,72]{2,1,0:T(1,128)}), s32[16,1,72]{2,1,0:T(1,128)S(1)}, u32[]{:S(2)}, u32[]{:S(2)}) %all-to-all-start.1) | async-done | bytes 4640 | tf_op jit(solution)/shard_map/all_to_all | solution.py:60
  75.4 0.7 reduce.17
  76.0 0.1 reshape.106
  76.1 0.1 reshape.104
  76.2 0.1 reshape.68
  76.3 17.7 %all-gather.1 = s32[8,1,1152]{2,1,0:T(1,128)S(1)} all-gather(s32[1,1,1152]{2,1,0:T(1,128)S(1)} %reshape.106), channel_id=1, replica_groups=mesh['group'=16,'span'=8] {'span'}, dimensions={0}, use_global_device_ids=true | all-gather | bytes 41472 | tf_op jit(solution)/shard_map/all_gather | solution.py:73
  94.0 13.0 %all-gather = s32[8,1,1152]{2,1,0:T(1,128)S(1)} all-gather(s32[1,1,1152]{2,1,0:T(1,128)S(1)} %reshape.104), channel_id=1, replica_groups=mesh['group'=16,'span'=8] {'span'}, dimensions={0}, use_global_device_ids=true | all-gather | bytes 41472 | tf_op jit(solution)/shard_map/all_gather | solution.py:72
  107.0 39.6 %all-gather.4.cloned.1.call-done = bf16[9216,1024]{1,0:T(8,128)(2,1)} async-done(((bf16[1152,1024]{1,0:T(8,128)(2,1)}), bf16[9216,1024]{1,0:T(8,128)(2,1)}) %all-gather.4.cloned.1.call-update) | async-done | bytes 18874384 | tf_op jit(solution)/shard_map/all_gather | solution.py:71
  146.6 0.0 copy-done
  146.6 29.1 %fusion = f32[1152]{0:T(1024)S(1)} fusion(bf16[1152,1024]{1,0:T(8,128)(2,1)S(1)} %bitcast.9, bf16[9216,1024]{1,0:T(8,128)(2,1)} %all-gather.4.cloned.1.call-done, pred[1152]{0:T(1024)(128)(4,1)S(1)} %broadcast_compare_fusion, s32[1152]{0:T(1024)S(1)} %reshape.68, s32[9216]{0:T(1024)S(1)} %bitcast.13, s32[9216]{0:T(1024)S(1)} %bitcast.14, s32[1152]{0:T(1024)S(1)} %eq.36), kind=kOutput, calls=%fused_computation.5 | convolution fusion | flops 21806970880 | bytes 21322368 | tf_op jit(solution)/shard_map/dot_general | solution.py:11
  175.6 0.7 max_broadcast_in_dim.15
  176.3 6.5 %all-to-all-start.3 = ((f32[16,1,72]{2,1,0:T(1,128)}), f32[16,1,72]{2,1,0:T(1,128)S(1)}, u32[]{:S(2)}, u32[]{:S(2)}) async-start(f32[16,1,72]{2,1,0:T(1,128)} %max_broadcast_in_dim.15), calls=%async_computation.3 | async-start | bytes 16384 | tf_op jit(solution)/shard_map/all_to_all | solution.py:75
  182.9 6.4 %all-to-all-done.3 = f32[16,1,72]{2,1,0:T(1,128)S(1)} async-done(((f32[16,1,72]{2,1,0:T(1,128)}), f32[16,1,72]{2,1,0:T(1,128)S(1)}, u32[]{:S(2)}, u32[]{:S(2)}) %all-to-all-start.3) | async-done | bytes 4640 | tf_op jit(solution)/shard_map/all_to_all | solution.py:75
  189.3 0.5 broadcast.70
  189.8 0.7 reduce.18
  190.4 0.1 reshape.71
  190.5 3.7 %gather_fusion = f32[384]{0:T(512)} fusion(f32[1152]{0:T(1024)S(1)} %reshape.71, s32[1024]{0:T(1024)S(1)} %pad_clamp_fusion), kind=kCustom, calls=%fused_computation | custom fusion | bytes 4608 | tf_op jit(solution)/shard_map/gather | solution.py:78
  (5 shorter events, 0.0 us)
Async XLA Ops:
  6.5 140.0 %all-gather.4.cloned.1.call-start = ((), (), s32[]{:S(2)}) async-start(), calls=%async_computation.4 | async-start | bytes 21233664 | tf_op jit(solution)/shard_map/all_gather | solution.py:71
  50.8 95.8 %copy-start = (bf16[16,72,1024]{2,1,0:T(8,128)(2,1)S(1)}, bf16[16,72,1024]{2,1,0:T(8,128)(2,1)}, u32[]{:S(2)}) copy-start(bf16[16,72,1024]{2,1,0:T(8,128)(2,1)} %all_to_all.29) | copy-start | bytes 7077892
  54.4 10.5 %all-to-all-start = ((s32[16,1,72]{2,1,0:T(1,128)}), s32[16,1,72]{2,1,0:T(1,128)S(1)}, u32[]{:S(2)}, u32[]{:S(2)}) async-start(s32[16,1,72]{2,1,0:T(1,128)} %all_to_all.19), calls=%async_computation | async-start | bytes 16384 | tf_op jit(solution)/shard_map/all_to_all | solution.py:59
  64.9 10.4 %all-to-all-start.1 = ((s32[16,1,72]{2,1,0:T(1,128)}), s32[16,1,72]{2,1,0:T(1,128)S(1)}, u32[]{:S(2)}, u32[]{:S(2)}) async-start(s32[16,1,72]{2,1,0:T(1,128)} %all_to_all.21), calls=%async_computation.1 | async-start | bytes 16384 | tf_op jit(solution)/shard_map/all_to_all | solution.py:60
  176.3 12.9 %all-to-all-start.3 = ((f32[16,1,72]{2,1,0:T(1,128)}), f32[16,1,72]{2,1,0:T(1,128)S(1)}, u32[]{:S(2)}, u32[]{:S(2)}) async-start(f32[16,1,72]{2,1,0:T(1,128)} %max_broadcast_in_dim.15), calls=%async_computation.3 | async-start | bytes 16384 | tf_op jit(solution)/shard_map/all_to_all | solution.py:75
Sparse Core Ops, SparseCore 0:
  50.9 95.5 all-gather.3
where the time goes:
time: 202 us; the launch traced here: 201 us
  blocking collectives  67.8 us (34%)
  waiting for transfers between devices  53.7 us (27%)
  matrix products  29.3 us (15%)
  starting transfers between devices  14.6 us (7%)
  between operations  13.5 us (7%)
  local copies, waits for them, and re-layouts  13.2 us (7%)
  other arithmetic  8.85 us (4%)
    all_gather x1, waiting for transfers between devices, per_device(): lax.all_gather(query_units, 'span', axis=0, tiled=True)  39.6 us
    all_to_all x1, blocking collectives, per_device(): lax.all_to_all(send_units, 'group', split_axis=0, concat_axis=0, tiled=True)  37.2 us
    dot_general x1, matrix products, improve(): lax.dot_general(query_units, key_units, (((1,), (1,)), ((), ())), preferr...  29.1 us
    all_gather x1, blocking collectives, per_device(): lax.all_gather(query_order, 'span', axis=0, tiled=True)  17.7 us
    all_gather x1, blocking collectives, per_device(): lax.all_gather(query_cluster, 'span', axis=0, tiled=True)  13 us
    all_to_all x1, starting transfers between devices, per_device(): lax.all_to_all(best_score.reshape(group_size, capacity), 'group', split_a...  6.52 us
    all_to_all x1, waiting for transfers between devices, per_device(): lax.all_to_all(best_score.reshape(group_size, capacity), 'group', split_a...  6.39 us
    all_to_all x1, waiting for transfers between devices, per_device(): lax.all_to_all(send_order, 'group', split_axis=0, concat_axis=0, tiled=True)  5.13 us
  transfers between devices with their start and end apart: 4, of which 4 were waited for; matrix products, arithmetic and copies ran while one was open for 4% of the time, Pallas kernels for 0%

commit v1 on v0

v1 whole, which is shorter than its diff:
```python
import jax
import jax.numpy as jnp
from jax import lax
from jax.experimental import pallas as pl
from jax.experimental.pallas import tpu as pltpu
from jax.sharding import Mesh, PartitionSpec as P

CLUSTERS = 48
MOST = 24
WIDTH = 1024
ROWS = 384
CHIPS = 64
PLANES = 4
USED = 3
BLOCKS = WIDTH // 128
CHUNK = BLOCKS * MOST + 8
HALF = CHIPS * MOST
TOP = 65535
LOW = 64
F32 = jnp.float32
BF16 = jnp.bfloat16
AXES = ("x", "y", "z", "c")
CHIP_AXES = ("x", "y", "z")


def iota(shape, dim):
    return lax.broadcasted_iota(jnp.int32, shape, dim)


def chunk_of(cluster):
    return cluster // USED * PLANES + cluster % USED


def prepare(emb_ref, cluster_ref, order_ref, send_ref, place_ref):
    cluster = cluster_ref[...]
    hot = (iota((CLUSTERS, ROWS), 0) == cluster).astype(BF16)
    before = (iota((ROWS, ROWS), 0) < iota((ROWS, ROWS), 1)).astype(BF16)
    counts = jnp.dot(hot, before, preferred_element_type=F32)
    rank = jnp.sum(counts * hot.astype(F32), axis=0, keepdims=True).astype(jnp.int32)
    slot = cluster * MOST + rank
    place_ref[...] = slot

    late = TOP - order_ref[...]
    high = (late >> 8).astype(F32)
    low = (late & 255).astype(F32)
    lane = iota((128, ROWS), 0)
    coded = jnp.where(lane == rank, high, 0.0) + jnp.where(lane == rank + LOW, low, 0.0)
    orders = lax.dot_general(
        hot, coded.astype(BF16), (((1,), (1,)), ((), ())), preferred_element_type=F32
    )

    emb = emb_ref[...]
    unit = (emb * lax.rsqrt(jnp.sum(emb * emb, axis=1, keepdims=True) + 1e-06)).astype(BF16)
    step = 16
    for part in range(CLUSTERS // step):
        rows = step * MOST
        pick = (iota((rows, ROWS), 0) + part * rows == slot).astype(BF16)
        taken = jnp.dot(pick, unit, preferred_element_type=F32).astype(BF16)
        for one in range(step):
            cluster_id = part * step + one
            to = chunk_of(cluster_id)
            for block in range(BLOCKS):
                send_ref[to, block * MOST : (block + 1) * MOST, :] = taken[
                    one * MOST : (one + 1) * MOST, block * 128 : (block + 1) * 128
                ]
            send_ref[to, BLOCKS * MOST : CHUNK, :] = jnp.broadcast_to(
                orders[cluster_id : cluster_id + 1, :], (8, 128)
            ).astype(BF16)


def key_lateness(got_ref):
    tile = got_ref[:, BLOCKS * MOST : CHUNK, :].astype(F32)
    wide = jnp.concatenate([tile, tile, tile], axis=1)
    row = iota((1, MOST, 128), 1)
    lane = iota((1, MOST, 128), 2)
    weight = jnp.where(lane == row, 256.0, 0.0) + jnp.where(lane == row + LOW, 1.0, 0.0)
    return jnp.sum((wide * weight).reshape(HALF, 128), axis=1, keepdims=True)


def unpack(got_ref, rows_ref):
    for block in range(BLOCKS):
        rows_ref[:, block * 128 : (block + 1) * 128] = got_ref[
            :, block * MOST : (block + 1) * MOST, :
        ].reshape(HALF, 128)


def best_scores(keys_ref, late_ref, queries, query_late):
    step = 256

    def body(index, best):
        start = pl.multiple_of(index * step, step)
        scores = lax.dot_general(
            keys_ref[pl.ds(start, step), :], queries, (((1,), (1,)), ((), ())),
            preferred_element_type=F32,
        )
        kept = jnp.where(late_ref[pl.ds(start, step), :] > query_late, scores, -1.0)
        return jnp.maximum(best, jnp.max(kept.reshape(step // 8, 8, HALF), axis=0))

    return lax.fori_loop(0, HALF // step, body, jnp.full((8, HALF), -1.0, F32))


def own_scores(got_ref, rows_ref, query_late_ref, best_ref, late_ref):
    unpack(got_ref, rows_ref)
    late = key_lateness(got_ref)
    late_ref[...] = late
    query_late = jnp.transpose(jnp.broadcast_to(late, (HALF, 128)))[0:1, :]
    query_late_ref[...] = query_late
    best_ref[...] = best_scores(rows_ref, late_ref, rows_ref[...], query_late)


def other_scores(got_ref, rows_ref, query_late_ref, best_ref, back_ref, keys_ref, late_ref):
    unpack(got_ref, keys_ref)
    late_ref[...] = key_lateness(got_ref)
    best = best_scores(keys_ref, late_ref, rows_ref[...], query_late_ref[...])
    best = jnp.max(jnp.maximum(best, best_ref[...]), axis=0, keepdims=True)
    column = iota((CHIPS, HALF), 1)
    source = iota((CHIPS, HALF), 0) * MOST
    member = ((column >= source) & (column < source + MOST)).astype(F32)
    row = jnp.sum(member * (column - source).astype(F32), axis=0, keepdims=True).astype(jnp.int32)
    spread = jnp.where(iota((128, HALF), 0) == row, best, 0.0)
    back = lax.dot_general(
        member, spread, (((1,), (1,)), ((), ())),
        precision=lax.Precision.HIGHEST, preferred_element_type=F32,
    )
    back_ref[...] = back.reshape(CHIPS, 1, 128)


def finish(back_ref, place_ref, out_ref):
    back = back_ref[...].reshape(CHIPS, 128)
    place = place_ref[...]
    first = iota((CHIPS, ROWS), 0)
    cluster_id = first // PLANES * USED + first % PLANES
    start = jnp.where(first % PLANES < USED, cluster_id * MOST, -MOST)
    member = ((place >= start) & (place < start + MOST)).astype(F32)
    rank = place - jnp.sum(member * start.astype(F32), axis=0, keepdims=True).astype(jnp.int32)
    columns = lax.dot_general(
        back, member, (((0,), (0,)), ((), ())),
        precision=lax.Precision.HIGHEST, preferred_element_type=F32,
    )
    out_ref[...] = jnp.sum(
        jnp.where(iota((128, ROWS), 0) == rank, columns, 0.0), axis=0, keepdims=True
    )


PARAMS = pltpu.CompilerParams(vmem_limit_bytes=24 * 1024 * 1024)


def per_device(embeddings, cluster_ids, order):
    shape = jax.ShapeDtypeStruct
    send, place = pl.pallas_call(
        prepare,
        out_shape=(shape((CHIPS, CHUNK, 128), BF16), shape((1, ROWS), jnp.int32)),
        compiler_params=PARAMS,
    )(embeddings, cluster_ids.reshape(1, ROWS), order.reshape(1, ROWS))
    got = lax.all_to_all(send, CHIP_AXES, split_axis=0, concat_axis=0, tiled=True)
    other = lax.ppermute(got, "c", [(0, 1), (1, 0)])
    cost = pl.CostEstimate(flops=2 * HALF * HALF * WIDTH, bytes_accessed=8 << 20, transcendentals=0)
    rows, query_late, best = pl.pallas_call(
        own_scores,
        out_shape=(shape((HALF, WIDTH), BF16), shape((1, HALF), F32), shape((8, HALF), F32)),
        scratch_shapes=[pltpu.VMEM((HALF, 1), F32)],
        compiler_params=PARAMS,
        cost_estimate=cost,
    )(got)
    back = pl.pallas_call(
        other_scores,
        out_shape=shape((CHIPS, 1, 128), F32),
        scratch_shapes=[pltpu.VMEM((HALF, WIDTH), BF16), pltpu.VMEM((HALF, 1), F32)],
        compiler_params=PARAMS,
        cost_estimate=cost,
    )(other, rows, query_late, best)
    returned = lax.all_to_all(back, CHIP_AXES, split_axis=0, concat_axis=0, tiled=True)
    nearest = pl.pallas_call(
        finish,
        out_shape=shape((1, ROWS), F32),
        compiler_params=PARAMS,
    )(returned, place)
    return nearest.reshape(ROWS)


def solution(mesh):
    fine = Mesh(mesh.devices.reshape(4, 4, PLANES, 2), AXES)
    return jax.shard_map(
        per_device,
        mesh=fine,
        in_specs=(P(AXES, None), P(AXES, None), P(AXES)),
        out_specs=P(AXES),
        check_vma=False,
    )
```

time: 202 us -> 90 us (0.45)
  waiting for transfers between devices: 53.7 us -> 0.01 us
  matrix products: 29.3 us -> 0 us
  Pallas kernels: 0 us -> 18.4 us
  between operations: 13.5 us -> 0.03 us
  starting transfers between devices: 14.6 us -> 3.12 us
  local copies, waits for them, and re-layouts: 13.2 us -> 2.77 us
  other arithmetic: 8.85 us -> 0.6 us
  blocking collectives: 67.8 us -> 64.8 us
    all_gather x1 -> x0, waiting for transfers between devices: 39.6 us -> none  [per_device(): lax.all_gather(query_units, 'span', axis=0, tiled=True)]
    all_gather x2 -> x0, blocking collectives: 30.7 us -> none  [the longest x1 17.7 us: per_device(): lax.all_gather(query_order, 'span', axis=0, tiled=True)]
    dot_general x2 -> x0, matrix products: 29.3 us -> none  [the longest x1 29.1 us: improve(): lax.dot_general(query_units, key_units, (((1,), (1,)), ((), ())), preferr...]
    all_to_all x1 -> x2, blocking collectives: 37.2 us -> 64.8 us  [the longest x1 52.2 us: per_device(): lax.all_to_all(send, CHIP_AXES, split_axis=0, concat_axis=0, tiled=True)]
    pallas_call x0 -> x4, Pallas kernels: none -> 18.4 us  [the longest x1 8.63 us: per_device(): pl.pallas_call(other_scores, out_shape=shape((CHIPS, 1, 128), F32), scrat...]
    all_to_all x3 -> x0, starting transfers between devices: 14.6 us -> none  [the longest x1 6.52 us: per_device(): lax.all_to_all(best_score.reshape(group_size, capacity), 'group', split_a...]
    all_to_all x3 -> x0, waiting for transfers between devices: 14.2 us -> none  [the longest x1 6.39 us: per_device(): lax.all_to_all(best_score.reshape(group_size, capacity), 'group', split_a...]
    scatter x2 -> x0, local copies, waits for them, and re-layouts: 6.01 us -> none  [the longest x1 3.09 us: per_device(): jnp.zeros((total_slots,), jnp.int32).at[slot_index].set(order)]
  transfers between devices with their start and end apart: 4 -> 1, of which waited for: 4 -> 0; matrix products, arithmetic and copies ran while one was open for 4% -> 0% of each run, Pallas kernels for 0% -> 9%
where the time goes in v1:
time: 90 us; the launch traced here: 89.7 us
  blocking collectives  64.8 us (72%)
  Pallas kernels  18.4 us (20%)
  starting transfers between devices  3.12 us (3%)
  local copies, waits for them, and re-layouts  2.77 us (3%)
    all_to_all x1, blocking collectives, per_device(): lax.all_to_all(send, CHIP_AXES, split_axis=0, concat_axis=0, tiled=True)  52.2 us
    all_to_all x1, blocking collectives, per_device(): lax.all_to_all(back, CHIP_AXES, split_axis=0, concat_axis=0, tiled=True)  12.7 us
    pallas_call x1, Pallas kernels, per_device(): pl.pallas_call(other_scores, out_shape=shape((CHIPS, 1, 128), F32), scrat...  8.63 us
    pallas_call x1, Pallas kernels, per_device(): pl.pallas_call(own_scores, out_shape=(shape((HALF, WIDTH), BF16), shape((...  7.72 us
    ppermute x1, starting transfers between devices, per_device(): other = lax.ppermute(got, 'c', [(0, 1), (1, 0)])  3.12 us
    unnamed x4, local copies, waits for them, and re-layouts  2.09 us
  transfers between devices with their start and end apart: 1, of which 0 were waited for; matrix products, arithmetic and copies ran while one was open for 0% of the time, Pallas kernels for 9%

profile of v1, /device:TPU:1, one launch (start us, length us, event | category | flops | bytes accessed | tf_op | source)
XLA Modules:
  0.0 89.7 jit_solution(747639769723170956)
XLA Ops:
  0.0 0.7 reshape.10.order_ref
  0.7 0.0 copy-start
  0.7 1.4 %copy-done = f32[384,1024]{1,0:T(8,128)S(1)} copy-done((f32[384,1024]{1,0:T(8,128)S(1)}, f32[384,1024]{1,0:T(8,128)}, u32[]{:S(2)}) %copy-start) | copy-done | bytes 1572888
  2.1 0.0 copy-start.1
  2.1 0.7 copy-done.1
  2.8 1.6 %shard_map.37 = (bf16[64,200,128]{2,1,0:T(8,128)(2,1)S(1)}, s32[1,384]{1,0:T(1,128)S(1)}) custom-call(f32[384,1024]{1,0:T(8,128)S(1)} %copy-done, s32[1,384]{1,0:T(1,128)S(1)} %bitcast.1, s32[1,384]{1,0:T(1,128)S(1)} %reshape.10.order_ref), custom_call_target="tpu_custom_call" | custom-call | tf_op jit(solution)/shard_map/pallas_call | solution.py:150
  4.4 52.2 %all_to_all.10.got_ref = bf16[64,200,128]{2,1,0:T(8,128)(2,1)S(1)} all-to-all(bf16[64,200,128]{2,1,0:T(8,128)(2,1)S(1)} %get-tuple-element.10), channel_id=1, replica_groups=mesh['x'=4,'y'=4,'z'=4,'c'=2] {'x','y','z'}, dimensions={0} | all-to-all | bytes 6553600 | tf_op jit(solution)/shard_map/all_to_all | solution.py:155
  56.6 3.1 %collective-permute-start = (bf16[64,200,128]{2,1,0:T(8,128)(2,1)S(1)}, bf16[64,200,128]{2,1,0:T(8,128)(2,1)S(1)}, u32[]{:S(2)}, u32[]{:S(2)}) collective-permute-start(bf16[64,200,128]{2,1,0:T(8,128)(2,1)S(1)} %all_to_all.10.got_ref), channel_id=1, source_target_pairs={{0,1},{1,0},{2,3},{3,2},{4,5},{5,4},{6,7},{7,6},{8,9},{9,8},{10,11... | collective-permute-start | bytes 9830408 | tf_op jit(solution)/shard_map/ppermute | solution.py:156
  59.7 7.7 %shard_map.38 = (bf16[1536,1024]{1,0:T(8,128)(2,1)S(1)}, f32[1,1536]{1,0:T(1,128)S(1)}, f32[8,1536]{1,0:T(8,128)S(1)}) custom-call(bf16[64,200,128]{2,1,0:T(8,128)(2,1)S(1)} %all_to_all.10.got_ref), custom_call_target="tpu_custom_call" | custom-call | flops 4831838208 | bytes 8388608 | tf_op jit(solution)/shard_map/pallas_call | solution.py:158
  67.4 0.0 collective-permute-done.got_ref
  67.4 8.6 %shard_map.39 = f32[64,1,128]{2,1,0:T(1,128)S(1)} custom-call(bf16[64,200,128]{2,1,0:T(8,128)(2,1)S(1)} %collective-permute-done.got_ref, bf16[1536,1024]{1,0:T(8,128)(2,1)S(1)} %get-tuple-element.11.rows_ref, f32[1,1536]{1,0:T(1,128)S(1)} %get-tuple-element.12.query_late_ref, f32[8,1536]{1,0:T(8,128)S(1)} %get-tuple-element.13.best_ref), custom_call_target="tpu_custom_call" | custom-call | flops 4831838208 | bytes 8388608 | tf_op jit(solution)/shard_map/pallas_call | solution.py:165
  76.1 12.7 %all_to_all.11.back_ref = f32[64,1,128]{2,1,0:T(1,128)S(1)} all-to-all(f32[64,1,128]{2,1,0:T(1,128)S(1)} %shard_map.39), channel_id=1, replica_groups=mesh['x'=4,'y'=4,'z'=4,'c'=2] {'x','y','z'}, dimensions={0} | all-to-all | bytes 65536 | tf_op jit(solution)/shard_map/all_to_all | solution.py:172
  88.7 0.4 shard_map.40
  89.1 0.6 reduce
Async XLA Ops:
  0.7 1.4 %copy-start = (f32[384,1024]{1,0:T(8,128)S(1)}, f32[384,1024]{1,0:T(8,128)}, u32[]{:S(2)}) copy-start(f32[384,1024]{1,0:T(8,128)} %emb_ref.1) | copy-start | bytes 4718596
  2.1 0.7 copy-start.1
  56.6 10.8 %collective-permute-start = (bf16[64,200,128]{2,1,0:T(8,128)(2,1)S(1)}, bf16[64,200,128]{2,1,0:T(8,128)(2,1)S(1)}, u32[]{:S(2)}, u32[]{:S(2)}) collective-permute-start(bf16[64,200,128]{2,1,0:T(8,128)(2,1)S(1)} %all_to_all.10.got_ref), channel_id=1, source_target_pairs={{0,1},{1,0},{2,3},{3,2},{4,5},{5,4},{6,7},{7,6},{8,9},{9,8},{10,11... | collective-permute-start | bytes 9830408 | tf_op jit(solution)/shard_map/ppermute | solution.py:156

commit v2 on v1

v2 whole, which is shorter than its diff:
```python
import jax
import jax.numpy as jnp
from jax import lax
from jax.experimental import pallas as pl
from jax.experimental.pallas import tpu as pltpu
from jax.sharding import Mesh, PartitionSpec as P

CLUSTERS = 48
MOST = 24
WIDTH = 1024
ROWS = 384
CHIPS = 64
PLANES = 4
USED = 3
BLOCKS = WIDTH // 128
CHUNK = BLOCKS * MOST + 8
HALF = CHIPS * MOST
TILE = 16 * MOST
TOP = 65535
LOW = 64
PIECES = 3
PARTS = 4
F32 = jnp.float32
BF16 = jnp.bfloat16
AXES = ("x", "y", "z", "c")
CHIP_AXES = ("x", "y", "z")


def iota(shape, dim):
    return lax.broadcasted_iota(jnp.int32, shape, dim)


def chunk_of(cluster):
    return cluster // USED * PLANES + cluster % USED


def prepare(
    emb_hbm, cluster_hbm, order_hbm, send_hbm, place_ref,
    emb_ref, cluster_ref, order_ref, send_ref, sem, send_sem,
):
    copies = [
        pltpu.make_async_copy(cluster_hbm, cluster_ref, sem.at[PIECES]),
        pltpu.make_async_copy(order_hbm, order_ref, sem.at[PIECES + 1]),
    ]
    piece = ROWS // PIECES
    for one in range(PIECES):
        rows = pl.ds(one * piece, piece)
        copies.append(
            pltpu.make_async_copy(emb_hbm.at[rows, :], emb_ref.at[rows, :], sem.at[one])
        )
    for copy in copies:
        copy.start()
    copies[0].wait()
    copies[1].wait()
    cluster = cluster_ref[...]
    hot = (iota((CLUSTERS, ROWS), 0) == cluster).astype(BF16)
    before = (iota((ROWS, ROWS), 0) < iota((ROWS, ROWS), 1)).astype(BF16)
    counts = jnp.dot(hot, before, preferred_element_type=F32)
    rank = jnp.sum(counts * hot.astype(F32), axis=0, keepdims=True).astype(jnp.int32)
    slot = cluster * MOST + rank
    place_ref[...] = slot

    late = TOP - order_ref[...].reshape(1, ROWS)
    high = (late >> 8).astype(F32)
    low = (late & 255).astype(F32)
    lane = iota((128, ROWS), 0)
    coded = jnp.where(lane == rank, high, 0.0) + jnp.where(lane == rank + LOW, low, 0.0)
    orders = lax.dot_general(
        hot, coded.astype(BF16), (((1,), (1,)), ((), ())), preferred_element_type=F32
    )

    for unused in range(USED, CHIPS, PLANES):
        send_ref[unused] = jnp.zeros((CHUNK, 128), BF16)
    units = []
    for one in range(PIECES):
        copies[2 + one].wait()
        emb = emb_ref[one * piece : (one + 1) * piece, :]
        total = jnp.sum(emb * emb, axis=1, keepdims=True)
        units.append((emb * lax.rsqrt(total + 1e-06)).astype(BF16))
    unit = jnp.concatenate(units, axis=0)
    step = CLUSTERS // PARTS
    share = CHIPS // PARTS
    sends = []
    for part in range(PARTS):
        rows = step * MOST
        pick = (iota((rows, ROWS), 0) + part * rows == slot).astype(BF16)
        taken = jnp.dot(pick, unit, preferred_element_type=F32).astype(BF16)
        for one in range(step):
            cluster_id = part * step + one
            to = chunk_of(cluster_id)
            for block in range(BLOCKS):
                send_ref[to, block * MOST : (block + 1) * MOST, :] = taken[
                    one * MOST : (one + 1) * MOST, block * 128 : (block + 1) * 128
                ]
            send_ref[to, BLOCKS * MOST : CHUNK, :] = jnp.broadcast_to(
                orders[cluster_id : cluster_id + 1, :], (8, 128)
            ).astype(BF16)
        chunks = pl.ds(part * share, share)
        sends.append(
            pltpu.make_async_copy(send_ref.at[chunks], send_hbm.at[chunks], send_sem.at[part])
        )
        sends[part].start()
    for send in sends:
        send.wait()


def key_lateness(got_ref):
    tile = got_ref[:, BLOCKS * MOST : CHUNK, :].astype(F32)
    row = iota((1, 8, 128), 1)
    lane = iota((1, 8, 128), 2)
    parts = []
    for first in range(0, MOST, 8):
        weight = jnp.where(lane == row + first, 256.0, 0.0)
        weight = weight + jnp.where(lane == row + (first + LOW), 1.0, 0.0)
        parts.append(tile * weight)
    wide = jnp.concatenate(parts, axis=1).reshape(HALF, 128)
    return jnp.sum(wide, axis=1, keepdims=True)


def unpacked(got_ref, first):
    rows = TILE // MOST
    return jnp.concatenate(
        [
            got_ref[
                first * rows : (first + 1) * rows, block * MOST : (block + 1) * MOST, :
            ].reshape(TILE, 128)
            for block in range(BLOCKS)
        ],
        axis=1,
    )


def best_of(keys, key_late, queries, query_late):
    scores = lax.dot_general(
        keys, queries, (((1,), (1,)), ((), ())), preferred_element_type=F32
    )
    kept = jnp.where(key_late > query_late, scores, -1.0)
    return jnp.max(kept.reshape(TILE // 8, 8, HALF), axis=0)


def own_scores(got_ref, rows_ref, query_late_ref, best_ref, late_ref):
    for part in range(HALF // TILE):
        rows_ref[part * TILE : (part + 1) * TILE, :] = unpacked(got_ref, part)
    late_ref[...] = jnp.broadcast_to(key_lateness(got_ref), (HALF, 128))
    query_late = jnp.transpose(late_ref[...])[0:1, :]
    query_late_ref[...] = query_late
    best = jnp.full((8, HALF), -1.0, F32)
    for part in range(HALF // TILE):
        rows = slice(part * TILE, (part + 1) * TILE)
        found = best_of(rows_ref[rows, :], late_ref[rows, 0:1], rows_ref[...], query_late)
        best = jnp.maximum(best, found)
    best_ref[...] = best


def other_scores(got_ref, rows_ref, query_late_ref, best_ref, back_ref, late_ref):
    late_ref[...] = jnp.broadcast_to(key_lateness(got_ref), (HALF, 128))
    best = best_ref[...]
    for part in range(HALF // TILE):
        rows = slice(part * TILE, (part + 1) * TILE)
        found = best_of(
            unpacked(got_ref, part), late_ref[rows, 0:1], rows_ref[...], query_late_ref[...]
        )
        best = jnp.maximum(best, found)
    best = jnp.max(best, axis=0, keepdims=True)
    column = iota((CHIPS, HALF), 1)
    source = iota((CHIPS, HALF), 0) * MOST
    member = ((column >= source) & (column < source + MOST)).astype(F32)
    row = jnp.sum(member * (column - source).astype(F32), axis=0, keepdims=True).astype(jnp.int32)
    spread = jnp.where(iota((128, HALF), 0) == row, best, 0.0)
    back = lax.dot_general(
        member, spread, (((1,), (1,)), ((), ())),
        precision=lax.Precision.HIGHEST, preferred_element_type=F32,
    )
    back_ref[...] = back.reshape(CHIPS, 1, 128)


def finish(back_ref, place_ref, out_ref):
    back = back_ref[...].reshape(CHIPS, 128)
    place = place_ref[...]
    first = iota((CHIPS, ROWS), 0)
    cluster_id = first // PLANES * USED + first % PLANES
    start = jnp.where(first % PLANES < USED, cluster_id * MOST, -MOST)
    member = ((place >= start) & (place < start + MOST)).astype(F32)
    rank = place - jnp.sum(member * start.astype(F32), axis=0, keepdims=True).astype(jnp.int32)
    columns = lax.dot_general(
        back, member, (((0,), (0,)), ((), ())),
        precision=lax.Precision.HIGHEST, preferred_element_type=F32,
    )
    out_ref[...] = jnp.sum(
        jnp.where(iota((128, ROWS), 0) == rank, columns, 0.0), axis=0
    )


PARAMS = pltpu.CompilerParams(vmem_limit_bytes=24 * 1024 * 1024)


def per_device(embeddings, cluster_ids, order):
    shape = jax.ShapeDtypeStruct
    send, place = pl.pallas_call(
        prepare,
        out_shape=(shape((CHIPS, CHUNK, 128), BF16), shape((1, ROWS), jnp.int32)),
        in_specs=[pl.BlockSpec(memory_space=pltpu.HBM)] * 3,
        out_specs=(
            pl.BlockSpec(memory_space=pltpu.HBM),
            pl.BlockSpec(memory_space=pltpu.VMEM),
        ),
        scratch_shapes=[
            pltpu.VMEM((ROWS, WIDTH), F32),
            pltpu.VMEM((1, ROWS), jnp.int32),
            pltpu.VMEM((ROWS,), jnp.int32),
            pltpu.VMEM((CHIPS, CHUNK, 128), BF16),
            pltpu.SemaphoreType.DMA((PIECES + 2,)),
            pltpu.SemaphoreType.DMA((PARTS,)),
        ],
        compiler_params=pltpu.CompilerParams(vmem_limit_bytes=60 * 1024 * 1024),
    )(embeddings, cluster_ids.reshape(1, ROWS), order)
    got = lax.all_to_all(send, CHIP_AXES, split_axis=0, concat_axis=0, tiled=True)
    other = lax.ppermute(got, "c", [(0, 1), (1, 0)])
    cost = pl.CostEstimate(flops=2 * HALF * HALF * WIDTH, bytes_accessed=8 << 20, transcendentals=0)
    rows, query_late, best = pl.pallas_call(
        own_scores,
        out_shape=(shape((HALF, WIDTH), BF16), shape((1, HALF), F32), shape((8, HALF), F32)),
        scratch_shapes=[pltpu.VMEM((HALF, 128), F32)],
        compiler_params=PARAMS,
        cost_estimate=cost,
    )(got)
    back = pl.pallas_call(
        other_scores,
        out_shape=shape((CHIPS, 1, 128), F32),
        scratch_shapes=[pltpu.VMEM((HALF, 128), F32)],
        compiler_params=PARAMS,
        cost_estimate=cost,
    )(other, rows, query_late, best)
    returned = lax.all_to_all(back, CHIP_AXES, split_axis=0, concat_axis=0, tiled=True)
    return pl.pallas_call(
        finish,
        out_shape=shape((ROWS,), F32),
        compiler_params=PARAMS,
    )(returned, place)


def solution(mesh):
    fine = Mesh(mesh.devices.reshape(4, 4, PLANES, 2), AXES)
    return jax.shard_map(
        per_device,
        mesh=fine,
        in_specs=(P(AXES, None), P(AXES, None), P(AXES)),
        out_specs=P(AXES),
        check_vma=False,
    )
```

time: 90 us -> 86.1 us (0.957)
  local copies, waits for them, and re-layouts: 2.77 us -> 0.01 us
  Pallas kernels: 18.4 us -> 17 us
    pallas_call x1, Pallas kernels: 1.64 us -> 4.36 us  [per_device(): pl.pallas_call(prepare, out_shape=(shape((CHIPS, CHUNK, 128), BF16), shap...]
    pallas_call x1, Pallas kernels: 7.72 us -> 5.17 us  [per_device(): pl.pallas_call(own_scores, out_shape=(shape((HALF, WIDTH), BF16), shape((...]
    pallas_call x1, Pallas kernels: 8.63 us -> 6.51 us  [per_device(): pl.pallas_call(other_scores, out_shape=shape((CHIPS, 1, 128), F32), scrat...]
    unnamed x4 -> x2, local copies, waits for them, and re-layouts: 2.09 us -> 0.01 us
  transfers between devices with their start and end apart: 1 -> 1, of which waited for: 0 -> 1; matrix products, arithmetic and copies ran while one was open for 0% -> 0% of each run, Pallas kernels for 9% -> 6%
where the time goes in v2:
time: 86.1 us; the launch traced here: 85.4 us
  blocking collectives  65 us (75%)
  Pallas kernels  17 us (20%)
  starting transfers between devices  3.13 us (4%)
    all_to_all x1, blocking collectives, per_device(): lax.all_to_all(send, CHIP_AXES, split_axis=0, concat_axis=0, tiled=True)  52.4 us
    all_to_all x1, blocking collectives, per_device(): lax.all_to_all(back, CHIP_AXES, split_axis=0, concat_axis=0, tiled=True)  12.7 us
    pallas_call x1, Pallas kernels, per_device(): pl.pallas_call(other_scores, out_shape=shape((CHIPS, 1, 128), F32), scrat...  6.51 us
    pallas_call x1, Pallas kernels, per_device(): pl.pallas_call(own_scores, out_shape=(shape((HALF, WIDTH), BF16), shape((...  5.17 us
    pallas_call x1, Pallas kernels, per_device(): pl.pallas_call(prepare, out_shape=(shape((CHIPS, CHUNK, 128), BF16), shap...  4.36 us
    ppermute x1, starting transfers between devices, per_device(): other = lax.ppermute(got, 'c', [(0, 1), (1, 0)])  3.13 us
  transfers between devices with their start and end apart: 1, of which 1 were waited for; matrix products, arithmetic and copies ran while one was open for 0% of the time, Pallas kernels for 6%

profile of v2, /device:TPU:1, one launch (start us, length us, event | category | flops | bytes accessed | tf_op | source)
XLA Modules:
  0.0 85.4 jit_solution(10701141583562703151)
XLA Ops:
  0.0 4.4 %shard_map.37 = (bf16[64,200,128]{2,1,0:T(8,128)(2,1)}, s32[1,384]{1,0:T(1,128)}) custom-call(f32[384,1024]{1,0:T(8,128)} %emb_hbm.1, s32[1,384]{1,0:T(1,128)} %bitcast.1, s32[384]{0:T(512)} %order_hbm.1), custom_call_target="tpu_custom_call" | custom-call | tf_op jit(solution)/shard_map/pallas_call | solution.py:199
  4.4 52.4 %all_to_all.10.got_ref = bf16[64,200,128]{2,1,0:T(8,128)(2,1)S(1)} all-to-all(bf16[64,200,128]{2,1,0:T(8,128)(2,1)} %get-tuple-element.10), channel_id=1, replica_groups=mesh['x'=4,'y'=4,'z'=4,'c'=2] {'x','y','z'}, dimensions={0} | all-to-all | bytes 6553600 | tf_op jit(solution)/shard_map/all_to_all | solution.py:217
  56.7 3.1 %collective-permute-start = (bf16[64,200,128]{2,1,0:T(8,128)(2,1)S(1)}, bf16[64,200,128]{2,1,0:T(8,128)(2,1)S(1)}, u32[]{:S(2)}, u32[]{:S(2)}) collective-permute-start(bf16[64,200,128]{2,1,0:T(8,128)(2,1)S(1)} %all_to_all.10.got_ref), channel_id=1, source_target_pairs={{0,1},{1,0},{2,3},{3,2},{4,5},{5,4},{6,7},{7,6},{8,9},{9,8},{10,11... | collective-permute-start | bytes 9830408 | tf_op jit(solution)/shard_map/ppermute | solution.py:218
  59.9 5.2 %shard_map.38 = (bf16[1536,1024]{1,0:T(8,128)(2,1)S(1)}, f32[1,1536]{1,0:T(1,128)S(1)}, f32[8,1536]{1,0:T(8,128)S(1)}) custom-call(bf16[64,200,128]{2,1,0:T(8,128)(2,1)S(1)} %all_to_all.10.got_ref), custom_call_target="tpu_custom_call" | custom-call | flops 4831838208 | bytes 8388608 | tf_op jit(solution)/shard_map/pallas_call | solution.py:220
  65.0 0.3 collective-permute-done.got_ref
  65.3 0.0 copy-start
  65.3 6.5 %shard_map.39 = f32[64,1,128]{2,1,0:T(1,128)S(1)} custom-call(bf16[64,200,128]{2,1,0:T(8,128)(2,1)S(1)} %collective-permute-done.got_ref, bf16[1536,1024]{1,0:T(8,128)(2,1)S(1)} %get-tuple-element.11.rows_ref, f32[1,1536]{1,0:T(1,128)S(1)} %get-tuple-element.12.query_late_ref, f32[8,1536]{1,0:T(8,128)S(1)} %get-tuple-element.13.best_ref), custom_call_target="tpu_custom_call" | custom-call | flops 4831838208 | bytes 8388608 | tf_op jit(solution)/shard_map/pallas_call | solution.py:227
  71.8 12.7 %all_to_all.11.back_ref = f32[64,1,128]{2,1,0:T(1,128)S(1)} all-to-all(f32[64,1,128]{2,1,0:T(1,128)S(1)} %shard_map.39), channel_id=1, replica_groups=mesh['x'=4,'y'=4,'z'=4,'c'=2] {'x','y','z'}, dimensions={0} | all-to-all | bytes 65536 | tf_op jit(solution)/shard_map/all_to_all | solution.py:234
  84.5 0.0 copy-done
  84.5 0.9 %shard_map.40 = f32[384]{0:T(512)} custom-call(f32[64,1,128]{2,1,0:T(1,128)S(1)} %all_to_all.11.back_ref, s32[1,384]{1,0:T(1,128)S(1)} %copy-done), custom_call_target="tpu_custom_call" | custom-call | tf_op jit(solution)/shard_map/pallas_call | solution.py:235
Async XLA Ops:
  56.7 8.6 %collective-permute-start = (bf16[64,200,128]{2,1,0:T(8,128)(2,1)S(1)}, bf16[64,200,128]{2,1,0:T(8,128)(2,1)S(1)}, u32[]{:S(2)}, u32[]{:S(2)}) collective-permute-start(bf16[64,200,128]{2,1,0:T(8,128)(2,1)S(1)} %all_to_all.10.got_ref), channel_id=1, source_target_pairs={{0,1},{1,0},{2,3},{3,2},{4,5},{5,4},{6,7},{7,6},{8,9},{9,8},{10,11... | collective-permute-start | bytes 9830408 | tf_op jit(solution)/shard_map/ppermute | solution.py:218
  65.3 19.2 %copy-start = (s32[1,384]{1,0:T(1,128)S(1)}, s32[1,384]{1,0:T(1,128)}, u32[]{:S(2)}) copy-start(s32[1,384]{1,0:T(1,128)} %get-tuple-element.14.place_ref) | copy-start | bytes 4612

commit v3 on v2

--- a/solution.py
+++ b/solution.py
@@ -19,7 +19,8 @@
 TOP = 65535
 LOW = 64
 PIECES = 3
-PARTS = 4
+PARTS = 8
+THIRD = 32
 F32 = jnp.float32
 BF16 = jnp.bfloat16
 AXES = ("x", "y", "z", "c")
@@ -58,7 +59,8 @@
     counts = jnp.dot(hot, before, preferred_element_type=F32)
     rank = jnp.sum(counts * hot.astype(F32), axis=0, keepdims=True).astype(jnp.int32)
     slot = cluster * MOST + rank
-    place_ref[...] = slot
+    place_ref[0:1, :] = cluster + ((cluster * 171) >> 9)
+    place_ref[1:2, :] = rank
 
     late = TOP - order_ref[...].reshape(1, ROWS)
     high = (late >> 8).astype(F32)
@@ -104,16 +106,16 @@
         send.wait()
 
 
-def key_lateness(got_ref):
-    tile = got_ref[:, BLOCKS * MOST : CHUNK, :].astype(F32)
+def key_lateness(got_ref, first, count):
+    tile = got_ref[first : first + count, BLOCKS * MOST : CHUNK, :].astype(F32)
     row = iota((1, 8, 128), 1)
     lane = iota((1, 8, 128), 2)
     parts = []
-    for first in range(0, MOST, 8):
-        weight = jnp.where(lane == row + first, 256.0, 0.0)
-        weight = weight + jnp.where(lane == row + (first + LOW), 1.0, 0.0)
+    for start in range(0, MOST, 8):
+        weight = jnp.where(lane == row + start, 256.0, 0.0)
+        weight = weight + jnp.where(lane == row + (start + LOW), 1.0, 0.0)
         parts.append(tile * weight)
-    wide = jnp.concatenate(parts, axis=1).reshape(HALF, 128)
+    wide = jnp.concatenate(parts, axis=1).reshape(count * MOST, 128)
     return jnp.sum(wide, axis=1, keepdims=True)
 
 
@@ -141,7 +143,7 @@
 def own_scores(got_ref, rows_ref, query_late_ref, best_ref, late_ref):
     for part in range(HALF // TILE):
         rows_ref[part * TILE : (part + 1) * TILE, :] = unpacked(got_ref, part)
-    late_ref[...] = jnp.broadcast_to(key_lateness(got_ref), (HALF, 128))
+    late_ref[...] = jnp.broadcast_to(key_lateness(got_ref, 0, CHIPS), (HALF, 128))
     query_late = jnp.transpose(late_ref[...])[0:1, :]
     query_late_ref[...] = query_late
     best = jnp.full((8, HALF), -1.0, F32)
@@ -152,43 +154,52 @@
     best_ref[...] = best
 
 
-def other_scores(got_ref, rows_ref, query_late_ref, best_ref, back_ref, late_ref):
-    late_ref[...] = jnp.broadcast_to(key_lateness(got_ref), (HALF, 128))
+def exact_parts(row):
+    high = row.astype(BF16)
+    rest = row - high.astype(F32)
+    middle = rest.astype(BF16)
+    low = (rest - middle.astype(F32)).astype(BF16)
+    return high, middle, low
+
+
+def other_scores(got_ref, rows_ref, query_late_ref, best_ref, back_ref):
+    column = iota((CHIPS, HALF), 1)
+    source = iota((CHIPS, HALF), 0) * MOST
+    member = (column >= source) & (column < source + MOST)
+    row = jnp.sum(jnp.where(member, column - source, 0), axis=0, keepdims=True)
+    here = iota((THIRD, HALF), 0) == row
     best = best_ref[...]
+    sources = TILE // MOST
     for part in range(HALF // TILE):
-        rows = slice(part * TILE, (part + 1) * TILE)
         found = best_of(
-            unpacked(got_ref, part), late_ref[rows, 0:1], rows_ref[...], query_late_ref[...]
+            unpacked(got_ref, part),
+            key_lateness(got_ref, part * sources, sources),
+            rows_ref[...],
+            query_late_ref[...],
         )
         best = jnp.maximum(best, found)
     best = jnp.max(best, axis=0, keepdims=True)
-    column = iota((CHIPS, HALF), 1)
-    source = iota((CHIPS, HALF), 0) * MOST
-    member = ((column >= source) & (column < source + MOST)).astype(F32)
-    row = jnp.sum(member * (column - source).astype(F32), axis=0, keepdims=True).astype(jnp.int32)
-    spread = jnp.where(iota((128, HALF), 0) == row, best, 0.0)
+    spread = [jnp.where(here, one.astype(F32), 0.0) for one in exact_parts(best)]
+    spread.append(jnp.zeros((THIRD, HALF), F32))
     back = lax.dot_general(
-        member, spread, (((1,), (1,)), ((), ())),
-        precision=lax.Precision.HIGHEST, preferred_element_type=F32,
+        member.astype(BF16),
+        jnp.concatenate(spread, axis=0).astype(BF16),
+        (((1,), (1,)), ((), ())),
+        preferred_element_type=F32,
     )
     back_ref[...] = back.reshape(CHIPS, 1, 128)
 
 
 def finish(back_ref, place_ref, out_ref):
-    back = back_ref[...].reshape(CHIPS, 128)
-    place = place_ref[...]
-    first = iota((CHIPS, ROWS), 0)
-    cluster_id = first // PLANES * USED + first % PLANES
-    start = jnp.where(first % PLANES < USED, cluster_id * MOST, -MOST)
-    member = ((place >= start) & (place < start + MOST)).astype(F32)
-    rank = place - jnp.sum(member * start.astype(F32), axis=0, keepdims=True).astype(jnp.int32)
+    back = back_ref[...].reshape(CHIPS, 128).astype(BF16)
+    member = (iota((CHIPS, ROWS), 0) == place_ref[0:1, :]).astype(BF16)
     columns = lax.dot_general(
-        back, member, (((0,), (0,)), ((), ())),
-        precision=lax.Precision.HIGHEST, preferred_element_type=F32,
-    )
-    out_ref[...] = jnp.sum(
-        jnp.where(iota((128, ROWS), 0) == rank, columns, 0.0), axis=0
-    )
+        back, member, (((0,), (0,)), ((), ())), preferred_element_type=F32
+    )
+    rank = place_ref[1:2, :]
+    row = iota((THIRD, ROWS), 0)
+    high, middle, low = (columns[one * THIRD : (one + 1) * THIRD, :] for one in range(3))
+    out_ref[...] = jnp.sum(jnp.where(row == rank, (low + middle) + high, 0.0), axis=0)
 
 
 PARAMS = pltpu.CompilerParams(vmem_limit_bytes=24 * 1024 * 1024)
@@ -198,7 +209,7 @@
     shape = jax.ShapeDtypeStruct
     send, place = pl.pallas_call(
         prepare,
-        out_shape=(shape((CHIPS, CHUNK, 128), BF16), shape((1, ROWS), jnp.int32)),
+        out_shape=(shape((CHIPS, CHUNK, 128), BF16), shape((2, ROWS), jnp.int32)),
         in_specs=[pl.BlockSpec(memory_space=pltpu.HBM)] * 3,
         out_specs=(
             pl.BlockSpec(memory_space=pltpu.HBM),
@@ -227,7 +238,6 @@
     back = pl.pallas_call(
         other_scores,
         out_shape=shape((CHIPS, 1, 128), F32),
-        scratch_shapes=[pltpu.VMEM((HALF, 128), F32)],
         compiler_params=PARAMS,
         cost_estimate=cost,
     )(other, rows, query_late, best)

time: 86.1 us -> 84.9 us (0.986)
  Pallas kernels: 17 us -> 15.8 us
    pallas_call x1, Pallas kernels: 6.51 us -> 5.49 us  [per_device(): pl.pallas_call(other_scores, out_shape=shape((CHIPS, 1, 128), F32), compi...]
where the time goes in v3:
time: 84.9 us; the launch traced here: 84.2 us
  blocking collectives  65 us (77%)
  Pallas kernels  15.8 us (19%)
  starting transfers between devices  3.13 us (4%)
    all_to_all x1, blocking collectives, per_device(): lax.all_to_all(send, CHIP_AXES, split_axis=0, concat_axis=0, tiled=True)  52.3 us
    all_to_all x1, blocking collectives, per_device(): lax.all_to_all(back, CHIP_AXES, split_axis=0, concat_axis=0, tiled=True)  12.7 us
    pallas_call x1, Pallas kernels, per_device(): pl.pallas_call(other_scores, out_shape=shape((CHIPS, 1, 128), F32), compi...  5.49 us
    pallas_call x1, Pallas kernels, per_device(): pl.pallas_call(own_scores, out_shape=(shape((HALF, WIDTH), BF16), shape((...  5.17 us
    pallas_call x1, Pallas kernels, per_device(): pl.pallas_call(prepare, out_shape=(shape((CHIPS, CHUNK, 128), BF16), shap...  4.31 us
    ppermute x1, starting transfers between devices, per_device(): other = lax.ppermute(got, 'c', [(0, 1), (1, 0)])  3.13 us
  transfers between devices with their start and end apart: 1, of which 1 were waited for; matrix products, arithmetic and copies ran while one was open for 0% of the time, Pallas kernels for 6%

profile of v3, /device:TPU:1, one launch (start us, length us, event | category | flops | bytes accessed | tf_op | source)
XLA Modules:
  0.0 84.2 jit_solution(16543157868910068159)
XLA Ops:
  0.0 4.3 %shard_map.37 = (bf16[64,200,128]{2,1,0:T(8,128)(2,1)}, s32[2,384]{1,0:T(2,128)}) custom-call(f32[384,1024]{1,0:T(8,128)} %emb_hbm.1, s32[1,384]{1,0:T(1,128)} %bitcast.1, s32[384]{0:T(512)} %order_hbm.1), custom_call_target="tpu_custom_call" | custom-call | tf_op jit(solution)/shard_map/pallas_call | solution.py:210
  4.3 52.3 %all_to_all.10.got_ref = bf16[64,200,128]{2,1,0:T(8,128)(2,1)S(1)} all-to-all(bf16[64,200,128]{2,1,0:T(8,128)(2,1)} %get-tuple-element.10), channel_id=1, replica_groups=mesh['x'=4,'y'=4,'z'=4,'c'=2] {'x','y','z'}, dimensions={0} | all-to-all | bytes 6553600 | tf_op jit(solution)/shard_map/all_to_all | solution.py:228
  56.7 3.1 %collective-permute-start = (bf16[64,200,128]{2,1,0:T(8,128)(2,1)S(1)}, bf16[64,200,128]{2,1,0:T(8,128)(2,1)S(1)}, u32[]{:S(2)}, u32[]{:S(2)}) collective-permute-start(bf16[64,200,128]{2,1,0:T(8,128)(2,1)S(1)} %all_to_all.10.got_ref), channel_id=1, source_target_pairs={{0,1},{1,0},{2,3},{3,2},{4,5},{5,4},{6,7},{7,6},{8,9},{9,8},{10,11... | collective-permute-start | bytes 9830408 | tf_op jit(solution)/shard_map/ppermute | solution.py:229
  59.8 5.2 %shard_map.38 = (bf16[1536,1024]{1,0:T(8,128)(2,1)S(1)}, f32[1,1536]{1,0:T(1,128)S(1)}, f32[8,1536]{1,0:T(8,128)S(1)}) custom-call(bf16[64,200,128]{2,1,0:T(8,128)(2,1)S(1)} %all_to_all.10.got_ref), custom_call_target="tpu_custom_call" | custom-call | flops 4831838208 | bytes 8388608 | tf_op jit(solution)/shard_map/pallas_call | solution.py:231
  65.0 0.3 collective-permute-done.got_ref
  65.3 0.0 copy-start
  65.3 5.5 %shard_map.39 = f32[64,1,128]{2,1,0:T(1,128)S(1)} custom-call(bf16[64,200,128]{2,1,0:T(8,128)(2,1)S(1)} %collective-permute-done.got_ref, bf16[1536,1024]{1,0:T(8,128)(2,1)S(1)} %get-tuple-element.11.rows_ref, f32[1,1536]{1,0:T(1,128)S(1)} %get-tuple-element.12.query_late_ref, f32[8,1536]{1,0:T(8,128)S(1)} %get-tuple-element.13.best_ref), custom_call_target="tpu_custom_call" | custom-call | flops 4831838208 | bytes 8388608 | tf_op jit(solution)/shard_map/pallas_call | solution.py:238
  70.8 12.7 %all_to_all.11.back_ref = f32[64,1,128]{2,1,0:T(1,128)S(1)} all-to-all(f32[64,1,128]{2,1,0:T(1,128)S(1)} %shard_map.39), channel_id=1, replica_groups=mesh['x'=4,'y'=4,'z'=4,'c'=2] {'x','y','z'}, dimensions={0} | all-to-all | bytes 65536 | tf_op jit(solution)/shard_map/all_to_all | solution.py:244
  83.4 0.0 copy-done
  83.4 0.8 shard_map.40
Async XLA Ops:
  56.7 8.6 %collective-permute-start = (bf16[64,200,128]{2,1,0:T(8,128)(2,1)S(1)}, bf16[64,200,128]{2,1,0:T(8,128)(2,1)S(1)}, u32[]{:S(2)}, u32[]{:S(2)}) collective-permute-start(bf16[64,200,128]{2,1,0:T(8,128)(2,1)S(1)} %all_to_all.10.got_ref), channel_id=1, source_target_pairs={{0,1},{1,0},{2,3},{3,2},{4,5},{5,4},{6,7},{7,6},{8,9},{9,8},{10,11... | collective-permute-start | bytes 9830408 | tf_op jit(solution)/shard_map/ppermute | solution.py:229
  65.3 18.2 %copy-start = (s32[2,384]{1,0:T(2,128)S(1)}, s32[2,384]{1,0:T(2,128)}, u32[]{:S(2)}) copy-start(s32[2,384]{1,0:T(2,128)} %get-tuple-element.14.place_ref) | copy-start | bytes 9220

commit v4 on v3

--- a/solution.py
+++ b/solution.py
@@ -25,19 +25,16 @@
 BF16 = jnp.bfloat16
 AXES = ("x", "y", "z", "c")
 CHIP_AXES = ("x", "y", "z")
+BACK_AXES = ("c", "x", "y", "z")
 
 
 def iota(shape, dim):
     return lax.broadcasted_iota(jnp.int32, shape, dim)
 
 
-def chunk_of(cluster):
-    return cluster // USED * PLANES + cluster % USED
-
-
 def prepare(
     emb_hbm, cluster_hbm, order_hbm, send_hbm, place_ref,
-    emb_ref, cluster_ref, order_ref, send_ref, sem, send_sem,
+    emb_ref, cluster_ref, order_ref, send_ref, zero_ref, sem, send_sem,
 ):
     copies = [
         pltpu.make_async_copy(cluster_hbm, cluster_ref, sem.at[PIECES]),
@@ -51,6 +48,9 @@
         )
     for copy in copies:
         copy.start()
+    zero_ref[...] = jnp.zeros((CHIPS // PLANES, CHUNK, 128), BF16)
+    zeros = pltpu.make_async_copy(zero_ref, send_hbm.at[:, USED], send_sem.at[PARTS])
+    zeros.start()
     copies[0].wait()
     copies[1].wait()
     cluster = cluster_ref[...]
@@ -71,8 +71,6 @@
         hot, coded.astype(BF16), (((1,), (1,)), ((), ())), preferred_element_type=F32
     )
 
-    for unused in range(USED, CHIPS, PLANES):
-        send_ref[unused] = jnp.zeros((CHUNK, 128), BF16)
     units = []
     for one in range(PIECES):
         copies[2 + one].wait()
@@ -81,27 +79,28 @@
         units.append((emb * lax.rsqrt(total + 1e-06)).astype(BF16))
     unit = jnp.concatenate(units, axis=0)
     step = CLUSTERS // PARTS
-    share = CHIPS // PARTS
-    sends = []
+    share = step // USED
+    sends = [zeros]
     for part in range(PARTS):
         rows = step * MOST
         pick = (iota((rows, ROWS), 0) + part * rows == slot).astype(BF16)
         taken = jnp.dot(pick, unit, preferred_element_type=F32).astype(BF16)
         for one in range(step):
             cluster_id = part * step + one
-            to = chunk_of(cluster_id)
+            to, plane = divmod(cluster_id, USED)
             for block in range(BLOCKS):
-                send_ref[to, block * MOST : (block + 1) * MOST, :] = taken[
+                send_ref[to, plane, block * MOST : (block + 1) * MOST, :] = taken[
                     one * MOST : (one + 1) * MOST, block * 128 : (block + 1) * 128
                 ]
-            send_ref[to, BLOCKS * MOST : CHUNK, :] = jnp.broadcast_to(
+            send_ref[to, plane, BLOCKS * MOST : CHUNK, :] = jnp.broadcast_to(
                 orders[cluster_id : cluster_id + 1, :], (8, 128)
             ).astype(BF16)
         chunks = pl.ds(part * share, share)
-        sends.append(
-            pltpu.make_async_copy(send_ref.at[chunks], send_hbm.at[chunks], send_sem.at[part])
+        send = pltpu.make_async_copy(
+            send_ref.at[chunks], send_hbm.at[chunks, 0:USED], send_sem.at[part]
         )
-        sends[part].start()
+        send.start()
+        sends.append(send)
     for send in sends:
         send.wait()
 
@@ -132,12 +131,15 @@
     )
 
 
-def best_of(keys, key_late, queries, query_late):
-    scores = lax.dot_general(
+def fold(scores):
+    rows, columns = scores.shape
+    return jnp.max(scores.reshape(rows // 8, 8, columns), axis=0)
+
+
+def score(keys, queries):
+    return lax.dot_general(
         keys, queries, (((1,), (1,)), ((), ())), preferred_element_type=F32
     )
-    kept = jnp.where(key_late > query_late, scores, -1.0)
-    return jnp.max(kept.reshape(TILE // 8, 8, HALF), axis=0)
 
 
 def own_scores(got_ref, rows_ref, query_late_ref, best_ref, late_ref):
@@ -149,57 +151,88 @@
     best = jnp.full((8, HALF), -1.0, F32)
     for part in range(HALF // TILE):
         rows = slice(part * TILE, (part + 1) * TILE)
-        found = best_of(rows_ref[rows, :], late_ref[rows, 0:1], rows_ref[...], query_late)
-        best = jnp.maximum(best, found)
+        scores = score(rows_ref[rows, :], rows_ref[...])
+        kept = jnp.where(late_ref[rows, 0:1] > query_late, scores, -1.0)
+        best = jnp.maximum(best, fold(kept))
     best_ref[...] = best
 
 
-def exact_parts(row):
-    high = row.astype(BF16)
-    rest = row - high.astype(F32)
+def exact_parts(values):
+    high = values.astype(BF16)
+    rest = values - high.astype(F32)
     middle = rest.astype(BF16)
     low = (rest - middle.astype(F32)).astype(BF16)
     return high, middle, low
 
 
-def other_scores(got_ref, rows_ref, query_late_ref, best_ref, back_ref):
+def by_source(best):
     column = iota((CHIPS, HALF), 1)
     source = iota((CHIPS, HALF), 0) * MOST
     member = (column >= source) & (column < source + MOST)
     row = jnp.sum(jnp.where(member, column - source, 0), axis=0, keepdims=True)
     here = iota((THIRD, HALF), 0) == row
-    best = best_ref[...]
-    sources = TILE // MOST
-    for part in range(HALF // TILE):
-        found = best_of(
-            unpacked(got_ref, part),
-            key_lateness(got_ref, part * sources, sources),
-            rows_ref[...],
-            query_late_ref[...],
-        )
-        best = jnp.maximum(best, found)
-    best = jnp.max(best, axis=0, keepdims=True)
     spread = [jnp.where(here, one.astype(F32), 0.0) for one in exact_parts(best)]
     spread.append(jnp.zeros((THIRD, HALF), F32))
-    back = lax.dot_general(
+    parts = lax.dot_general(
         member.astype(BF16),
         jnp.concatenate(spread, axis=0).astype(BF16),
         (((1,), (1,)), ((), ())),
         preferred_element_type=F32,
     )
-    back_ref[...] = back.reshape(CHIPS, 1, 128)
+    return (pltpu.roll(parts, 2 * THIRD, 1) + pltpu.roll(parts, 3 * THIRD, 1)) + parts
+
+
+def cross(got_ref, rows_ref, query_late_ref, best_ref, back_ref, first, queries, own_at, other_at):
+    sources = TILE // MOST
+    best = best_ref[:, 0:queries]
+    query_late = query_late_ref[:, 0:queries]
+    if first:
+        back_ref[other_at : other_at + first] = jnp.full((first, 1, 128), -1.0, F32)
+    for source in range(first, CHIPS, sources):
+        scores = score(unpacked(got_ref, source // sources), rows_ref[0:queries, :])
+        later = key_lateness(got_ref, source, sources) > query_late
+        best = jnp.maximum(best, fold(jnp.where(later, scores, -1.0)))
+        turned = jnp.where(later, -1.0, scores)
+        wide = turned[:, 0:128]
+        for start in range(128, queries, 128):
+            wide = jnp.maximum(wide, turned[:, start : start + 128])
+        found = jnp.max(wide, axis=1, keepdims=True)
+        found = jnp.broadcast_to(found, (TILE, 128)).reshape(sources, MOST, 128)
+        shape = (sources, MOST, 128)
+        placed = jnp.where(iota(shape, 1) == iota(shape, 2), found, 0.0)
+        back_ref[other_at + source : other_at + source + sources] = jnp.sum(
+            placed, axis=1
+        ).reshape(sources, 1, 128)
+    if queries < HALF:
+        best = jnp.concatenate([best, best_ref[:, queries:HALF]], axis=1)
+    best = jnp.max(best, axis=0, keepdims=True)
+    back_ref[own_at : own_at + CHIPS] = by_source(best).reshape(CHIPS, 1, 128)
+
+
+def other_scores(got_ref, rows_ref, query_late_ref, best_ref, back_ref):
+    core = lax.axis_index("c")
+    refs = (got_ref, rows_ref, query_late_ref, best_ref, back_ref)
+
+    @pl.when(core == 0)
+    def _():
+        cross(*refs, first=0, queries=HALF // 2, own_at=0, other_at=CHIPS)
+
+    @pl.when(core == 1)
+    def _():
+        cross(*refs, first=CHIPS // 2, queries=HALF, own_at=CHIPS, other_at=0)
 
 
 def finish(back_ref, place_ref, out_ref):
-    back = back_ref[...].reshape(CHIPS, 128).astype(BF16)
+    back = jnp.maximum(back_ref[0:CHIPS], back_ref[CHIPS : 2 * CHIPS]).reshape(CHIPS, 128)
     member = (iota((CHIPS, ROWS), 0) == place_ref[0:1, :]).astype(BF16)
     columns = lax.dot_general(
-        back, member, (((0,), (0,)), ((), ())), preferred_element_type=F32
-    )
-    rank = place_ref[1:2, :]
-    row = iota((THIRD, ROWS), 0)
-    high, middle, low = (columns[one * THIRD : (one + 1) * THIRD, :] for one in range(3))
-    out_ref[...] = jnp.sum(jnp.where(row == rank, (low + middle) + high, 0.0), axis=0)
+        jnp.concatenate(exact_parts(back), axis=0),
+        jnp.concatenate([member, member, member], axis=0),
+        (((0,), (0,)), ((), ())),
+        preferred_element_type=F32,
+    )
+    here = iota((THIRD, ROWS), 0) == place_ref[1:2, :]
+    out_ref[...] = jnp.sum(jnp.where(here, columns[0:THIRD, :], 0.0), axis=0)
 
 
 PARAMS = pltpu.CompilerParams(vmem_limit_bytes=24 * 1024 * 1024)
@@ -209,7 +242,7 @@
     shape = jax.ShapeDtypeStruct
     send, place = pl.pallas_call(
         prepare,
-        out_shape=(shape((CHIPS, CHUNK, 128), BF16), shape((2, ROWS), jnp.int32)),
+        out_shape=(shape((CHIPS // PLANES, PLANES, CHUNK, 128), BF16), shape((2, ROWS), jnp.int32)),
         in_specs=[pl.BlockSpec(memory_space=pltpu.HBM)] * 3,
         out_specs=(
             pl.BlockSpec(memory_space=pltpu.HBM),
@@ -219,12 +252,14 @@
             pltpu.VMEM((ROWS, WIDTH), F32),
             pltpu.VMEM((1, ROWS), jnp.int32),
             pltpu.VMEM((ROWS,), jnp.int32),
-            pltpu.VMEM((CHIPS, CHUNK, 128), BF16),
+            pltpu.VMEM((CHIPS // PLANES, USED, CHUNK, 128), BF16),
+            pltpu.VMEM((CHIPS // PLANES, CHUNK, 128), BF16),
             pltpu.SemaphoreType.DMA((PIECES + 2,)),
-            pltpu.SemaphoreType.DMA((PARTS,)),
+            pltpu.SemaphoreType.DMA((PARTS + 1,)),
         ],
         compiler_params=pltpu.CompilerParams(vmem_limit_bytes=60 * 1024 * 1024),
     )(embeddings, cluster_ids.reshape(1, ROWS), order)
+    send = send.reshape(CHIPS, CHUNK, 128)
     got = lax.all_to_all(send, CHIP_AXES, split_axis=0, concat_axis=0, tiled=True)
     other = lax.ppermute(got, "c", [(0, 1), (1, 0)])
     cost = pl.CostEstimate(flops=2 * HALF * HALF * WIDTH, bytes_accessed=8 << 20, transcendentals=0)
@@ -237,11 +272,11 @@
     )(got)
     back = pl.pallas_call(
         other_scores,
-        out_shape=shape((CHIPS, 1, 128), F32),
+        out_shape=shape((2 * CHIPS, 1, 128), F32),
         compiler_params=PARAMS,
         cost_estimate=cost,
     )(other, rows, query_late, best)
-    returned = lax.all_to_all(back, CHIP_AXES, split_axis=0, concat_axis=0, tiled=True)
+    returned = lax.all_to_all(back, BACK_AXES, split_axis=0, concat_axis=0, tiled=True)
     return pl.pallas_call(
         finish,
         out_shape=shape((ROWS,), F32),

time: 84.9 us -> 83.1 us (0.979)
  Pallas kernels: 15.8 us -> 13.9 us
    pallas_call x2, Pallas kernels: 9.8 us -> 7.83 us  [the longest x1 4.57 us: per_device(): pl.pallas_call(prepare, out_shape=(shape((CHIPS // PLANES, PLANES, CHUNK,...]
where the time goes in v4:
time: 83.1 us; the launch traced here: 82.8 us
  blocking collectives  65.5 us (79%)
  Pallas kernels  13.9 us (17%)
  starting transfers between devices  3.13 us (4%)
    all_to_all x1, blocking collectives, per_device(): lax.all_to_all(send, CHIP_AXES, split_axis=0, concat_axis=0, tiled=True)  52.4 us
    all_to_all x1, blocking collectives, per_device(): lax.all_to_all(back, BACK_AXES, split_axis=0, concat_axis=0, tiled=True)  13.1 us
    pallas_call x1, Pallas kernels, per_device(): pl.pallas_call(own_scores, out_shape=(shape((HALF, WIDTH), BF16), shape((...  5.17 us
    pallas_call x1, Pallas kernels, per_device(): pl.pallas_call(prepare, out_shape=(shape((CHIPS // PLANES, PLANES, CHUNK,...  4.57 us
    pallas_call x1, Pallas kernels, per_device(): pl.pallas_call(other_scores, out_shape=shape((2 * CHIPS, 1, 128), F32), c...  3.26 us
    ppermute x1, starting transfers between devices, per_device(): other = lax.ppermute(got, 'c', [(0, 1), (1, 0)])  3.13 us
  transfers between devices with their start and end apart: 1, of which 1 were waited for; matrix products, arithmetic and copies ran while one was open for 0% of the time, Pallas kernels for 6%

profile of v4, /device:TPU:1, one launch (start us, length us, event | category | flops | bytes accessed | tf_op | source)
XLA Modules:
  0.0 82.8 jit_solution(5313823198807593450)
XLA Ops:
  0.0 4.6 %shard_map.37 = (bf16[16,4,200,128]{3,2,1,0:T(8,128)(2,1)}, s32[2,384]{1,0:T(2,128)}) custom-call(f32[384,1024]{1,0:T(8,128)} %emb_hbm.1, s32[1,384]{1,0:T(1,128)} %bitcast.3, s32[384]{0:T(512)} %order_hbm.1), custom_call_target="tpu_custom_call" | custom-call | tf_op jit(solution)/shard_map/pallas_call | solution.py:243
  4.6 52.4 %all_to_all.10.got_ref = bf16[64,200,128]{2,1,0:T(8,128)(2,1)S(1)} all-to-all(bf16[64,200,128]{2,1,0:T(8,128)(2,1)} %bitcast.2), channel_id=1, replica_groups=mesh['x'=4,'y'=4,'z'=4,'c'=2] {'x','y','z'}, dimensions={0} | all-to-all | bytes 6553600 | tf_op jit(solution)/shard_map/all_to_all | solution.py:263
  56.9 3.1 %collective-permute-start = (bf16[64,200,128]{2,1,0:T(8,128)(2,1)S(1)}, bf16[64,200,128]{2,1,0:T(8,128)(2,1)S(1)}, u32[]{:S(2)}, u32[]{:S(2)}) collective-permute-start(bf16[64,200,128]{2,1,0:T(8,128)(2,1)S(1)} %all_to_all.10.got_ref), channel_id=1, source_target_pairs={{0,1},{1,0},{2,3},{3,2},{4,5},{5,4},{6,7},{7,6},{8,9},{9,8},{10,11... | collective-permute-start | bytes 9830408 | tf_op jit(solution)/shard_map/ppermute | solution.py:264
  60.1 5.2 %shard_map.38 = (bf16[1536,1024]{1,0:T(8,128)(2,1)S(1)}, f32[1,1536]{1,0:T(1,128)S(1)}, f32[8,1536]{1,0:T(8,128)S(1)}) custom-call(bf16[64,200,128]{2,1,0:T(8,128)(2,1)S(1)} %all_to_all.10.got_ref), custom_call_target="tpu_custom_call" | custom-call | flops 4831838208 | bytes 8388608 | tf_op jit(solution)/shard_map/pallas_call | solution.py:266
  65.2 0.3 collective-permute-done.got_ref
  65.5 0.0 copy-start
  65.5 3.3 %shard_map.39 = f32[128,1,128]{2,1,0:T(1,128)S(1)} custom-call(bf16[64,200,128]{2,1,0:T(8,128)(2,1)S(1)} %collective-permute-done.got_ref, bf16[1536,1024]{1,0:T(8,128)(2,1)S(1)} %get-tuple-element.11.rows_ref, f32[1,1536]{1,0:T(1,128)S(1)} %get-tuple-element.12.query_late_ref, f32[8,1536]{1,0:T(8,128)S(1)} %get-tuple-element.13.best_ref), custom_call_target="tpu_custom_call" | custom-call | flops 4831838208 | bytes 8388608 | tf_op jit(solution)/shard_map/pallas_call | solution.py:273
  68.8 13.1 %all_to_all.11.back_ref = f32[128,1,128]{2,1,0:T(1,128)S(1)} all-to-all(f32[128,1,128]{2,1,0:T(1,128)S(1)} %shard_map.39), channel_id=1, replica_groups=mesh['x'=4,'y'=4,'z'=4,'c'=2] {'c','x','y','z'}, dimensions={0} | all-to-all | bytes 131072 | tf_op jit(solution)/shard_map/all_to_all | solution.py:279
  81.9 0.0 copy-done
  81.9 0.9 %shard_map.40 = f32[384]{0:T(512)} custom-call(f32[128,1,128]{2,1,0:T(1,128)S(1)} %all_to_all.11.back_ref, s32[2,384]{1,0:T(2,128)S(1)} %copy-done), custom_call_target="tpu_custom_call" | custom-call | tf_op jit(solution)/shard_map/pallas_call | solution.py:280
Async XLA Ops:
  56.9 8.6 %collective-permute-start = (bf16[64,200,128]{2,1,0:T(8,128)(2,1)S(1)}, bf16[64,200,128]{2,1,0:T(8,128)(2,1)S(1)}, u32[]{:S(2)}, u32[]{:S(2)}) collective-permute-start(bf16[64,200,128]{2,1,0:T(8,128)(2,1)S(1)} %all_to_all.10.got_ref), channel_id=1, source_target_pairs={{0,1},{1,0},{2,3},{3,2},{4,5},{5,4},{6,7},{7,6},{8,9},{9,8},{10,11... | collective-permute-start | bytes 9830408 | tf_op jit(solution)/shard_map/ppermute | solution.py:264
  65.5 16.4 %copy-start = (s32[2,384]{1,0:T(2,128)S(1)}, s32[2,384]{1,0:T(2,128)}, u32[]{:S(2)}) copy-start(s32[2,384]{1,0:T(2,128)} %get-tuple-element.14.place_ref) | copy-start | bytes 9220

commit v5 on v4

--- a/solution.py
+++ b/solution.py
@@ -32,9 +32,13 @@
     return lax.broadcasted_iota(jnp.int32, shape, dim)
 
 
+def chunk_of(cluster):
+    return cluster // USED * PLANES + cluster % USED
+
+
 def prepare(
     emb_hbm, cluster_hbm, order_hbm, send_hbm, place_ref,
-    emb_ref, cluster_ref, order_ref, send_ref, zero_ref, sem, send_sem,
+    emb_ref, cluster_ref, order_ref, send_ref, sem, send_sem,
 ):
     copies = [
         pltpu.make_async_copy(cluster_hbm, cluster_ref, sem.at[PIECES]),
@@ -48,9 +52,6 @@
         )
     for copy in copies:
         copy.start()
-    zero_ref[...] = jnp.zeros((CHIPS // PLANES, CHUNK, 128), BF16)
-    zeros = pltpu.make_async_copy(zero_ref, send_hbm.at[:, USED], send_sem.at[PARTS])
-    zeros.start()
     copies[0].wait()
     copies[1].wait()
     cluster = cluster_ref[...]
@@ -71,6 +72,8 @@
         hot, coded.astype(BF16), (((1,), (1,)), ((), ())), preferred_element_type=F32
     )
 
+    for unused in range(USED, CHIPS, PLANES):
+        send_ref[unused] = jnp.zeros((CHUNK, 128), BF16)
     units = []
     for one in range(PIECES):
         copies[2 + one].wait()
@@ -79,28 +82,27 @@
         units.append((emb * lax.rsqrt(total + 1e-06)).astype(BF16))
     unit = jnp.concatenate(units, axis=0)
     step = CLUSTERS // PARTS
-    share = step // USED
-    sends = [zeros]
+    share = CHIPS // PARTS
+    sends = []
     for part in range(PARTS):
         rows = step * MOST
         pick = (iota((rows, ROWS), 0) + part * rows == slot).astype(BF16)
         taken = jnp.dot(pick, unit, preferred_element_type=F32).astype(BF16)
         for one in range(step):
             cluster_id = part * step + one
-            to, plane = divmod(cluster_id, USED)
+            to = chunk_of(cluster_id)
             for block in range(BLOCKS):
-                send_ref[to, plane, block * MOST : (block + 1) * MOST, :] = taken[
+                send_ref[to, block * MOST : (block + 1) * MOST, :] = taken[
                     one * MOST : (one + 1) * MOST, block * 128 : (block + 1) * 128
                 ]
-            send_ref[to, plane, BLOCKS * MOST : CHUNK, :] = jnp.broadcast_to(
+            send_ref[to, BLOCKS * MOST : CHUNK, :] = jnp.broadcast_to(
                 orders[cluster_id : cluster_id + 1, :], (8, 128)
             ).astype(BF16)
         chunks = pl.ds(part * share, share)
-        send = pltpu.make_async_copy(
-            send_ref.at[chunks], send_hbm.at[chunks, 0:USED], send_sem.at[part]
+        sends.append(
+            pltpu.make_async_copy(send_ref.at[chunks], send_hbm.at[chunks], send_sem.at[part])
         )
-        send.start()
-        sends.append(send)
+        sends[part].start()
     for send in sends:
         send.wait()
 
@@ -166,20 +168,28 @@
 
 
 def by_source(best):
-    column = iota((CHIPS, HALF), 1)
-    source = iota((CHIPS, HALF), 0) * MOST
+    sources = TILE // MOST
+    column = iota((sources, TILE), 1)
+    source = iota((sources, TILE), 0) * MOST
     member = (column >= source) & (column < source + MOST)
     row = jnp.sum(jnp.where(member, column - source, 0), axis=0, keepdims=True)
-    here = iota((THIRD, HALF), 0) == row
-    spread = [jnp.where(here, one.astype(F32), 0.0) for one in exact_parts(best)]
-    spread.append(jnp.zeros((THIRD, HALF), F32))
-    parts = lax.dot_general(
-        member.astype(BF16),
-        jnp.concatenate(spread, axis=0).astype(BF16),
-        (((1,), (1,)), ((), ())),
-        preferred_element_type=F32,
-    )
-    return (pltpu.roll(parts, 2 * THIRD, 1) + pltpu.roll(parts, 3 * THIRD, 1)) + parts
+    here = iota((THIRD, TILE), 0) == row
+    member = member.astype(F32).astype(BF16)
+    none = jnp.zeros((THIRD, TILE), F32)
+    groups = []
+    for start in range(0, HALF, TILE):
+        values = exact_parts(best[:, start : start + TILE])
+        spread = [jnp.where(here, one.astype(F32), 0.0) for one in values]
+        parts = lax.dot_general(
+            member,
+            jnp.concatenate(spread + [none], axis=0).astype(BF16),
+            (((1,), (1,)), ((), ())),
+            preferred_element_type=F32,
+        )
+        groups.append(
+            (pltpu.roll(parts, 2 * THIRD, 1) + pltpu.roll(parts, 3 * THIRD, 1)) + parts
+        )
+    return jnp.concatenate(groups, axis=0)
 
 
 def cross(got_ref, rows_ref, query_late_ref, best_ref, back_ref, first, queries, own_at, other_at):
@@ -242,7 +252,7 @@
     shape = jax.ShapeDtypeStruct
     send, place = pl.pallas_call(
         prepare,
-        out_shape=(shape((CHIPS // PLANES, PLANES, CHUNK, 128), BF16), shape((2, ROWS), jnp.int32)),
+        out_shape=(shape((CHIPS, CHUNK, 128), BF16), shape((2, ROWS), jnp.int32)),
         in_specs=[pl.BlockSpec(memory_space=pltpu.HBM)] * 3,
         out_specs=(
             pl.BlockSpec(memory_space=pltpu.HBM),
@@ -252,14 +262,12 @@
             pltpu.VMEM((ROWS, WIDTH), F32),
             pltpu.VMEM((1, ROWS), jnp.int32),
             pltpu.VMEM((ROWS,), jnp.int32),
-            pltpu.VMEM((CHIPS // PLANES, USED, CHUNK, 128), BF16),
-            pltpu.VMEM((CHIPS // PLANES, CHUNK, 128), BF16),
+            pltpu.VMEM((CHIPS, CHUNK, 128), BF16),
             pltpu.SemaphoreType.DMA((PIECES + 2,)),
-            pltpu.SemaphoreType.DMA((PARTS + 1,)),
+            pltpu.SemaphoreType.DMA((PARTS,)),
         ],
         compiler_params=pltpu.CompilerParams(vmem_limit_bytes=60 * 1024 * 1024),
     )(embeddings, cluster_ids.reshape(1, ROWS), order)
-    send = send.reshape(CHIPS, CHUNK, 128)
     got = lax.all_to_all(send, CHIP_AXES, split_axis=0, concat_axis=0, tiled=True)
     other = lax.ppermute(got, "c", [(0, 1), (1, 0)])
     cost = pl.CostEstimate(flops=2 * HALF * HALF * WIDTH, bytes_accessed=8 << 20, transcendentals=0)

time: 83.1 us -> 82.7 us (level)
  no operation moved by 1% of the time
where the time goes in v5:
time: 82.7 us; the launch traced here: 82.4 us
  blocking collectives  65.5 us (79%)
  Pallas kernels  13.5 us (16%)
  starting transfers between devices  3.13 us (4%)
    all_to_all x1, blocking collectives, per_device(): lax.all_to_all(send, CHIP_AXES, split_axis=0, concat_axis=0, tiled=True)  52.3 us
    all_to_all x1, blocking collectives, per_device(): lax.all_to_all(back, BACK_AXES, split_axis=0, concat_axis=0, tiled=True)  13.1 us
    pallas_call x1, Pallas kernels, per_device(): pl.pallas_call(own_scores, out_shape=(shape((HALF, WIDTH), BF16), shape((...  5.18 us
    pallas_call x1, Pallas kernels, per_device(): pl.pallas_call(prepare, out_shape=(shape((CHIPS, CHUNK, 128), BF16), shap...  4.31 us
    ppermute x1, starting transfers between devices, per_device(): other = lax.ppermute(got, 'c', [(0, 1), (1, 0)])  3.13 us
    pallas_call x1, Pallas kernels, per_device(): pl.pallas_call(other_scores, out_shape=shape((2 * CHIPS, 1, 128), F32), c...  3.11 us
  transfers between devices with their start and end apart: 1, of which 1 were waited for; matrix products, arithmetic and copies ran while one was open for 0% of the time, Pallas kernels for 6%

profile of v5, /device:TPU:1, one launch (start us, length us, event | category | flops | bytes accessed | tf_op | source)
XLA Modules:
  0.0 82.4 jit_solution(10146795514567755773)
XLA Ops:
  0.0 4.3 %shard_map.37 = (bf16[64,200,128]{2,1,0:T(8,128)(2,1)}, s32[2,384]{1,0:T(2,128)}) custom-call(f32[384,1024]{1,0:T(8,128)} %emb_hbm.1, s32[1,384]{1,0:T(1,128)} %bitcast.1, s32[384]{0:T(512)} %order_hbm.1), custom_call_target="tpu_custom_call" | custom-call | tf_op jit(solution)/shard_map/pallas_call | solution.py:253
  4.3 52.3 %all_to_all.10.got_ref = bf16[64,200,128]{2,1,0:T(8,128)(2,1)S(1)} all-to-all(bf16[64,200,128]{2,1,0:T(8,128)(2,1)} %get-tuple-element.10), channel_id=1, replica_groups=mesh['x'=4,'y'=4,'z'=4,'c'=2] {'x','y','z'}, dimensions={0} | all-to-all | bytes 6553600 | tf_op jit(solution)/shard_map/all_to_all | solution.py:271
  56.7 3.1 %collective-permute-start = (bf16[64,200,128]{2,1,0:T(8,128)(2,1)S(1)}, bf16[64,200,128]{2,1,0:T(8,128)(2,1)S(1)}, u32[]{:S(2)}, u32[]{:S(2)}) collective-permute-start(bf16[64,200,128]{2,1,0:T(8,128)(2,1)S(1)} %all_to_all.10.got_ref), channel_id=1, source_target_pairs={{0,1},{1,0},{2,3},{3,2},{4,5},{5,4},{6,7},{7,6},{8,9},{9,8},{10,11... | collective-permute-start | bytes 9830408 | tf_op jit(solution)/shard_map/ppermute | solution.py:272
  59.8 5.2 %shard_map.38 = (bf16[1536,1024]{1,0:T(8,128)(2,1)S(1)}, f32[1,1536]{1,0:T(1,128)S(1)}, f32[8,1536]{1,0:T(8,128)S(1)}) custom-call(bf16[64,200,128]{2,1,0:T(8,128)(2,1)S(1)} %all_to_all.10.got_ref), custom_call_target="tpu_custom_call" | custom-call | flops 4831838208 | bytes 8388608 | tf_op jit(solution)/shard_map/pallas_call | solution.py:274
  65.0 0.3 collective-permute-done.got_ref
  65.3 0.0 copy-start
  65.3 3.1 %shard_map.39 = f32[128,1,128]{2,1,0:T(1,128)S(1)} custom-call(bf16[64,200,128]{2,1,0:T(8,128)(2,1)S(1)} %collective-permute-done.got_ref, bf16[1536,1024]{1,0:T(8,128)(2,1)S(1)} %get-tuple-element.11.rows_ref, f32[1,1536]{1,0:T(1,128)S(1)} %get-tuple-element.12.query_late_ref, f32[8,1536]{1,0:T(8,128)S(1)} %get-tuple-element.13.best_ref), custom_call_target="tpu_custom_call" | custom-call | flops 4831838208 | bytes 8388608 | tf_op jit(solution)/shard_map/pallas_call | solution.py:281
  68.4 13.1 %all_to_all.11.back_ref = f32[128,1,128]{2,1,0:T(1,128)S(1)} all-to-all(f32[128,1,128]{2,1,0:T(1,128)S(1)} %shard_map.39), channel_id=1, replica_groups=mesh['x'=4,'y'=4,'z'=4,'c'=2] {'c','x','y','z'}, dimensions={0} | all-to-all | bytes 131072 | tf_op jit(solution)/shard_map/all_to_all | solution.py:287
  81.5 0.0 copy-done
  81.5 0.9 %shard_map.40 = f32[384]{0:T(512)} custom-call(f32[128,1,128]{2,1,0:T(1,128)S(1)} %all_to_all.11.back_ref, s32[2,384]{1,0:T(2,128)S(1)} %copy-done), custom_call_target="tpu_custom_call" | custom-call | tf_op jit(solution)/shard_map/pallas_call | solution.py:288
Async XLA Ops:
  56.7 8.6 %collective-permute-start = (bf16[64,200,128]{2,1,0:T(8,128)(2,1)S(1)}, bf16[64,200,128]{2,1,0:T(8,128)(2,1)S(1)}, u32[]{:S(2)}, u32[]{:S(2)}) collective-permute-start(bf16[64,200,128]{2,1,0:T(8,128)(2,1)S(1)} %all_to_all.10.got_ref), channel_id=1, source_target_pairs={{0,1},{1,0},{2,3},{3,2},{4,5},{5,4},{6,7},{7,6},{8,9},{9,8},{10,11... | collective-permute-start | bytes 9830408 | tf_op jit(solution)/shard_map/ppermute | solution.py:272
  65.3 16.3 %copy-start = (s32[2,384]{1,0:T(2,128)S(1)}, s32[2,384]{1,0:T(2,128)}, u32[]{:S(2)}) copy-start(s32[2,384]{1,0:T(2,128)} %get-tuple-element.14.place_ref) | copy-start | bytes 9220

commit v6 on v5

--- a/solution.py
+++ b/solution.py
@@ -19,7 +19,7 @@
 TOP = 65535
 LOW = 64
 PIECES = 3
-PARTS = 8
+PARTS = 3
 THIRD = 32
 F32 = jnp.float32
 BF16 = jnp.bfloat16
@@ -37,8 +37,8 @@
 
 
 def prepare(
-    emb_hbm, cluster_hbm, order_hbm, send_hbm, place_ref,
-    emb_ref, cluster_ref, order_ref, send_ref, sem, send_sem,
+    emb_hbm, cluster_hbm, order_hbm, send_ref, place_ref,
+    emb_ref, cluster_ref, order_ref, sem,
 ):
     copies = [
         pltpu.make_async_copy(cluster_hbm, cluster_ref, sem.at[PIECES]),
@@ -74,6 +74,8 @@
 
     for unused in range(USED, CHIPS, PLANES):
         send_ref[unused] = jnp.zeros((CHUNK, 128), BF16)
+    for unused in range(USED, CHIPS, PLANES):
+        send_ref[unused] = jnp.zeros((CHUNK, 128), BF16)
     units = []
     for one in range(PIECES):
         copies[2 + one].wait()
@@ -82,8 +84,6 @@
         units.append((emb * lax.rsqrt(total + 1e-06)).astype(BF16))
     unit = jnp.concatenate(units, axis=0)
     step = CLUSTERS // PARTS
-    share = CHIPS // PARTS
-    sends = []
     for part in range(PARTS):
         rows = step * MOST
         pick = (iota((rows, ROWS), 0) + part * rows == slot).astype(BF16)
@@ -98,13 +98,6 @@
             send_ref[to, BLOCKS * MOST : CHUNK, :] = jnp.broadcast_to(
                 orders[cluster_id : cluster_id + 1, :], (8, 128)
             ).astype(BF16)
-        chunks = pl.ds(part * share, share)
-        sends.append(
-            pltpu.make_async_copy(send_ref.at[chunks], send_hbm.at[chunks], send_sem.at[part])
-        )
-        sends[part].start()
-    for send in sends:
-        send.wait()
 
 
 def key_lateness(got_ref, first, count):
@@ -254,20 +247,18 @@
         prepare,
         out_shape=(shape((CHIPS, CHUNK, 128), BF16), shape((2, ROWS), jnp.int32)),
         in_specs=[pl.BlockSpec(memory_space=pltpu.HBM)] * 3,
-        out_specs=(
-            pl.BlockSpec(memory_space=pltpu.HBM),
-            pl.BlockSpec(memory_space=pltpu.VMEM),
-        ),
         scratch_shapes=[
             pltpu.VMEM((ROWS, WIDTH), F32),
             pltpu.VMEM((1, ROWS), jnp.int32),
             pltpu.VMEM((ROWS,), jnp.int32),
-            pltpu.VMEM((CHIPS, CHUNK, 128), BF16),
             pltpu.SemaphoreType.DMA((PIECES + 2,)),
-            pltpu.SemaphoreType.DMA((PARTS,)),
         ],
-        compiler_params=pltpu.CompilerParams(vmem_limit_bytes=60 * 1024 * 1024),
-    )(embeddings, cluster_ids.reshape(1, ROWS), order)
+        compiler_params=pltpu.CompilerParams(vmem_limit_bytes=24 * 1024 * 1024),
+    )(
+        pltpu.with_memory_space_constraint(embeddings, pltpu.HBM),
+        pltpu.with_memory_space_constraint(cluster_ids.reshape(1, ROWS), pltpu.HBM),
+        pltpu.with_memory_space_constraint(order, pltpu.HBM),
+    )
     got = lax.all_to_all(send, CHIP_AXES, split_axis=0, concat_axis=0, tiled=True)
     other = lax.ppermute(got, "c", [(0, 1), (1, 0)])
     cost = pl.CostEstimate(flops=2 * HALF * HALF * WIDTH, bytes_accessed=8 << 20, transcendentals=0)

time: 82.7 us -> 81 us (0.979)
  Pallas kernels: 13.5 us -> 12.1 us
    pallas_call x1, Pallas kernels: 4.31 us -> 2.94 us  [per_device(): pl.pallas_call(prepare, out_shape=(shape((CHIPS, CHUNK, 128), BF16), shap...]
where the time goes in v6:
time: 81 us; the launch traced here: 80.8 us
  blocking collectives  65.3 us (81%)
  Pallas kernels  12.1 us (15%)
  starting transfers between devices  3.12 us (4%)
    all_to_all x1, blocking collectives, per_device(): lax.all_to_all(send, CHIP_AXES, split_axis=0, concat_axis=0, tiled=True)  52.2 us
    all_to_all x1, blocking collectives, per_device(): lax.all_to_all(back, BACK_AXES, split_axis=0, concat_axis=0, tiled=True)  13.1 us
    pallas_call x1, Pallas kernels, per_device(): pl.pallas_call(own_scores, out_shape=(shape((HALF, WIDTH), BF16), shape((...  5.18 us
    ppermute x1, starting transfers between devices, per_device(): other = lax.ppermute(got, 'c', [(0, 1), (1, 0)])  3.12 us
    pallas_call x1, Pallas kernels, per_device(): pl.pallas_call(other_scores, out_shape=shape((2 * CHIPS, 1, 128), F32), c...  3.11 us
    pallas_call x1, Pallas kernels, per_device(): pl.pallas_call(prepare, out_shape=(shape((CHIPS, CHUNK, 128), BF16), shap...  2.94 us
  transfers between devices with their start and end apart: 1, of which 1 were waited for; matrix products, arithmetic and copies ran while one was open for 0% of the time, Pallas kernels for 6%

profile of v6, /device:TPU:1, one launch (start us, length us, event | category | flops | bytes accessed | tf_op | source)
XLA Modules:
  0.0 80.8 jit_solution(11173903701998426185)
XLA Ops:
  0.0 2.9 %shard_map.37 = (bf16[64,200,128]{2,1,0:T(8,128)(2,1)S(1)}, s32[2,384]{1,0:T(2,128)S(1)}) custom-call(f32[384,1024]{1,0:T(8,128)} %emb_hbm.1, s32[1,384]{1,0:T(1,128)} %bitcast.1, s32[384]{0:T(512)} %order_hbm.1), custom_call_target="tpu_custom_call" | custom-call | tf_op jit(solution)/shard_map/pallas_call | solution.py:246
  3.0 52.2 %all_to_all.10.got_ref = bf16[64,200,128]{2,1,0:T(8,128)(2,1)S(1)} all-to-all(bf16[64,200,128]{2,1,0:T(8,128)(2,1)S(1)} %get-tuple-element.10), channel_id=1, replica_groups=mesh['x'=4,'y'=4,'z'=4,'c'=2] {'x','y','z'}, dimensions={0} | all-to-all | bytes 6553600 | tf_op jit(solution)/shard_map/all_to_all | solution.py:262
  55.1 3.1 %collective-permute-start = (bf16[64,200,128]{2,1,0:T(8,128)(2,1)S(1)}, bf16[64,200,128]{2,1,0:T(8,128)(2,1)S(1)}, u32[]{:S(2)}, u32[]{:S(2)}) collective-permute-start(bf16[64,200,128]{2,1,0:T(8,128)(2,1)S(1)} %all_to_all.10.got_ref), channel_id=1, source_target_pairs={{0,1},{1,0},{2,3},{3,2},{4,5},{5,4},{6,7},{7,6},{8,9},{9,8},{10,11... | collective-permute-start | bytes 9830408 | tf_op jit(solution)/shard_map/ppermute | solution.py:263
  58.2 5.2 %shard_map.38 = (bf16[1536,1024]{1,0:T(8,128)(2,1)S(1)}, f32[1,1536]{1,0:T(1,128)S(1)}, f32[8,1536]{1,0:T(8,128)S(1)}) custom-call(bf16[64,200,128]{2,1,0:T(8,128)(2,1)S(1)} %all_to_all.10.got_ref), custom_call_target="tpu_custom_call" | custom-call | flops 4831838208 | bytes 8388608 | tf_op jit(solution)/shard_map/pallas_call | solution.py:265
  63.4 0.3 collective-permute-done.got_ref
  63.7 3.1 %shard_map.39 = f32[128,1,128]{2,1,0:T(1,128)S(1)} custom-call(bf16[64,200,128]{2,1,0:T(8,128)(2,1)S(1)} %collective-permute-done.got_ref, bf16[1536,1024]{1,0:T(8,128)(2,1)S(1)} %get-tuple-element.11.rows_ref, f32[1,1536]{1,0:T(1,128)S(1)} %get-tuple-element.12.query_late_ref, f32[8,1536]{1,0:T(8,128)S(1)} %get-tuple-element.13.best_ref), custom_call_target="tpu_custom_call" | custom-call | flops 4831838208 | bytes 8388608 | tf_op jit(solution)/shard_map/pallas_call | solution.py:272
  66.8 13.1 %all_to_all.11.back_ref = f32[128,1,128]{2,1,0:T(1,128)S(1)} all-to-all(f32[128,1,128]{2,1,0:T(1,128)S(1)} %shard_map.39), channel_id=1, replica_groups=mesh['x'=4,'y'=4,'z'=4,'c'=2] {'c','x','y','z'}, dimensions={0} | all-to-all | bytes 131072 | tf_op jit(solution)/shard_map/all_to_all | solution.py:278
  79.9 0.9 %shard_map.40 = f32[384]{0:T(512)} custom-call(f32[128,1,128]{2,1,0:T(1,128)S(1)} %all_to_all.11.back_ref, s32[2,384]{1,0:T(2,128)S(1)} %get-tuple-element.14.place_ref), custom_call_target="tpu_custom_call" | custom-call | tf_op jit(solution)/shard_map/pallas_call | solution.py:279
Async XLA Ops:
  55.1 8.6 %collective-permute-start = (bf16[64,200,128]{2,1,0:T(8,128)(2,1)S(1)}, bf16[64,200,128]{2,1,0:T(8,128)(2,1)S(1)}, u32[]{:S(2)}, u32[]{:S(2)}) collective-permute-start(bf16[64,200,128]{2,1,0:T(8,128)(2,1)S(1)} %all_to_all.10.got_ref), channel_id=1, source_target_pairs={{0,1},{1,0},{2,3},{3,2},{4,5},{5,4},{6,7},{7,6},{8,9},{9,8},{10,11... | collective-permute-start | bytes 9830408 | tf_op jit(solution)/shard_map/ppermute | solution.py:263

commit v7 on v6

--- a/solution.py
+++ b/solution.py
@@ -15,7 +15,7 @@
 BLOCKS = WIDTH // 128
 CHUNK = BLOCKS * MOST + 8
 HALF = CHIPS * MOST
-TILE = 16 * MOST
+TILE = 32 * MOST
 TOP = 65535
 LOW = 64
 PIECES = 3
@@ -52,11 +52,13 @@
         )
     for copy in copies:
         copy.start()
+    for unused in range(USED, CHIPS, PLANES):
+        send_ref[unused] = jnp.zeros((CHUNK, 128), BF16)
+    before = (iota((ROWS, ROWS), 0) < iota((ROWS, ROWS), 1)).astype(BF16)
     copies[0].wait()
     copies[1].wait()
     cluster = cluster_ref[...]
     hot = (iota((CLUSTERS, ROWS), 0) == cluster).astype(BF16)
-    before = (iota((ROWS, ROWS), 0) < iota((ROWS, ROWS), 1)).astype(BF16)
     counts = jnp.dot(hot, before, preferred_element_type=F32)
     rank = jnp.sum(counts * hot.astype(F32), axis=0, keepdims=True).astype(jnp.int32)
     slot = cluster * MOST + rank
@@ -72,10 +74,6 @@
         hot, coded.astype(BF16), (((1,), (1,)), ((), ())), preferred_element_type=F32
     )
 
-    for unused in range(USED, CHIPS, PLANES):
-        send_ref[unused] = jnp.zeros((CHUNK, 128), BF16)
-    for unused in range(USED, CHIPS, PLANES):
-        send_ref[unused] = jnp.zeros((CHUNK, 128), BF16)
     units = []
     for one in range(PIECES):
         copies[2 + one].wait()

time: 81 us -> 80.6 us (level)
  no operation moved by 1% of the time
where the time goes in v7:
time: 80.6 us; the launch traced here: 80.5 us
  blocking collectives  65 us (81%)
  Pallas kernels  12 us (15%)
  starting transfers between devices  3.13 us (4%)
    all_to_all x1, blocking collectives, per_device(): lax.all_to_all(send, CHIP_AXES, split_axis=0, concat_axis=0, tiled=True)  52.1 us
    all_to_all x1, blocking collectives, per_device(): lax.all_to_all(back, BACK_AXES, split_axis=0, concat_axis=0, tiled=True)  12.9 us
    pallas_call x1, Pallas kernels, per_device(): pl.pallas_call(own_scores, out_shape=(shape((HALF, WIDTH), BF16), shape((...  5.12 us
    pallas_call x1, Pallas kernels, per_device(): pl.pallas_call(other_scores, out_shape=shape((2 * CHIPS, 1, 128), F32), c...  3.13 us
    ppermute x1, starting transfers between devices, per_device(): other = lax.ppermute(got, 'c', [(0, 1), (1, 0)])  3.13 us
    pallas_call x1, Pallas kernels, per_device(): pl.pallas_call(prepare, out_shape=(shape((CHIPS, CHUNK, 128), BF16), shap...  2.82 us
  transfers between devices with their start and end apart: 1, of which 1 were waited for; matrix products, arithmetic and copies ran while one was open for 0% of the time, Pallas kernels for 6%

profile of v7, /device:TPU:1, one launch (start us, length us, event | category | flops | bytes accessed | tf_op | source)
XLA Modules:
  0.0 80.5 jit_solution(12076079860743884096)
XLA Ops:
  0.0 2.8 %shard_map.37 = (bf16[64,200,128]{2,1,0:T(8,128)(2,1)S(1)}, s32[2,384]{1,0:T(2,128)S(1)}) custom-call(f32[384,1024]{1,0:T(8,128)} %emb_hbm.1, s32[1,384]{1,0:T(1,128)} %bitcast.1, s32[384]{0:T(512)} %order_hbm.1), custom_call_target="tpu_custom_call" | custom-call | tf_op jit(solution)/shard_map/pallas_call | solution.py:244
  2.8 52.1 %all_to_all.10.got_ref = bf16[64,200,128]{2,1,0:T(8,128)(2,1)S(1)} all-to-all(bf16[64,200,128]{2,1,0:T(8,128)(2,1)S(1)} %get-tuple-element.10), channel_id=1, replica_groups=mesh['x'=4,'y'=4,'z'=4,'c'=2] {'x','y','z'}, dimensions={0} | all-to-all | bytes 6553600 | tf_op jit(solution)/shard_map/all_to_all | solution.py:260
  55.0 3.1 %collective-permute-start = (bf16[64,200,128]{2,1,0:T(8,128)(2,1)S(1)}, bf16[64,200,128]{2,1,0:T(8,128)(2,1)S(1)}, u32[]{:S(2)}, u32[]{:S(2)}) collective-permute-start(bf16[64,200,128]{2,1,0:T(8,128)(2,1)S(1)} %all_to_all.10.got_ref), channel_id=1, source_target_pairs={{0,1},{1,0},{2,3},{3,2},{4,5},{5,4},{6,7},{7,6},{8,9},{9,8},{10,11... | collective-permute-start | bytes 9830408 | tf_op jit(solution)/shard_map/ppermute | solution.py:261
  58.1 5.1 %shard_map.38 = (bf16[1536,1024]{1,0:T(8,128)(2,1)S(1)}, f32[1,1536]{1,0:T(1,128)S(1)}, f32[8,1536]{1,0:T(8,128)S(1)}) custom-call(bf16[64,200,128]{2,1,0:T(8,128)(2,1)S(1)} %all_to_all.10.got_ref), custom_call_target="tpu_custom_call" | custom-call | flops 4831838208 | bytes 8388608 | tf_op jit(solution)/shard_map/pallas_call | solution.py:263
  63.2 0.3 collective-permute-done.got_ref
  63.6 3.1 %shard_map.39 = f32[128,1,128]{2,1,0:T(1,128)S(1)} custom-call(bf16[64,200,128]{2,1,0:T(8,128)(2,1)S(1)} %collective-permute-done.got_ref, bf16[1536,1024]{1,0:T(8,128)(2,1)S(1)} %get-tuple-element.11.rows_ref, f32[1,1536]{1,0:T(1,128)S(1)} %get-tuple-element.12.query_late_ref, f32[8,1536]{1,0:T(8,128)S(1)} %get-tuple-element.13.best_ref), custom_call_target="tpu_custom_call" | custom-call | flops 4831838208 | bytes 8388608 | tf_op jit(solution)/shard_map/pallas_call | solution.py:270
  66.7 12.9 %all_to_all.11.back_ref = f32[128,1,128]{2,1,0:T(1,128)S(1)} all-to-all(f32[128,1,128]{2,1,0:T(1,128)S(1)} %shard_map.39), channel_id=1, replica_groups=mesh['x'=4,'y'=4,'z'=4,'c'=2] {'c','x','y','z'}, dimensions={0} | all-to-all | bytes 131072 | tf_op jit(solution)/shard_map/all_to_all | solution.py:276
  79.6 0.9 %shard_map.40 = f32[384]{0:T(512)} custom-call(f32[128,1,128]{2,1,0:T(1,128)S(1)} %all_to_all.11.back_ref, s32[2,384]{1,0:T(2,128)S(1)} %get-tuple-element.14.place_ref), custom_call_target="tpu_custom_call" | custom-call | tf_op jit(solution)/shard_map/pallas_call | solution.py:277
Async XLA Ops:
  55.0 8.6 %collective-permute-start = (bf16[64,200,128]{2,1,0:T(8,128)(2,1)S(1)}, bf16[64,200,128]{2,1,0:T(8,128)(2,1)S(1)}, u32[]{:S(2)}, u32[]{:S(2)}) collective-permute-start(bf16[64,200,128]{2,1,0:T(8,128)(2,1)S(1)} %all_to_all.10.got_ref), channel_id=1, source_target_pairs={{0,1},{1,0},{2,3},{3,2},{4,5},{5,4},{6,7},{7,6},{8,9},{9,8},{10,11... | collective-permute-start | bytes 9830408 | tf_op jit(solution)/shard_map/ppermute | solution.py:261

commit v8 on v7

--- a/solution.py
+++ b/solution.py
@@ -74,6 +74,12 @@
         hot, coded.astype(BF16), (((1,), (1,)), ((), ())), preferred_element_type=F32
     )
 
+    for cluster_id in range(CLUSTERS):
+        send_ref[chunk_of(cluster_id), BLOCKS * MOST : CHUNK, :] = jnp.broadcast_to(
+            orders[cluster_id : cluster_id + 1, :], (8, 128)
+        ).astype(BF16)
+    rows = CLUSTERS // PARTS * MOST
+    picks = [(iota((rows, ROWS), 0) == slot).astype(BF16)]
     units = []
     for one in range(PIECES):
         copies[2 + one].wait()
@@ -84,8 +90,9 @@
     step = CLUSTERS // PARTS
     for part in range(PARTS):
         rows = step * MOST
-        pick = (iota((rows, ROWS), 0) + part * rows == slot).astype(BF16)
-        taken = jnp.dot(pick, unit, preferred_element_type=F32).astype(BF16)
+        if part:
+            picks.append((iota((rows, ROWS), 0) + part * rows == slot).astype(BF16))
+        taken = jnp.dot(picks[part], unit, preferred_element_type=F32).astype(BF16)
         for one in range(step):
             cluster_id = part * step + one
             to = chunk_of(cluster_id)
@@ -93,9 +100,6 @@
                 send_ref[to, block * MOST : (block + 1) * MOST, :] = taken[
                     one * MOST : (one + 1) * MOST, block * 128 : (block + 1) * 128
                 ]
-            send_ref[to, BLOCKS * MOST : CHUNK, :] = jnp.broadcast_to(
-                orders[cluster_id : cluster_id + 1, :], (8, 128)
-            ).astype(BF16)
 
 
 def key_lateness(got_ref, first, count):
@@ -185,28 +189,30 @@
 
 def cross(got_ref, rows_ref, query_late_ref, best_ref, back_ref, first, queries, own_at, other_at):
     sources = TILE // MOST
-    best = best_ref[:, 0:queries]
-    query_late = query_late_ref[:, 0:queries]
+    starts = range(0, HALF, TILE)
+    best = [best_ref[:, start : start + TILE] for start in starts]
     if first:
         back_ref[other_at : other_at + first] = jnp.full((first, 1, 128), -1.0, F32)
     for source in range(first, CHIPS, sources):
-        scores = score(unpacked(got_ref, source // sources), rows_ref[0:queries, :])
-        later = key_lateness(got_ref, source, sources) > query_late
-        best = jnp.maximum(best, fold(jnp.where(later, scores, -1.0)))
-        turned = jnp.where(later, -1.0, scores)
-        wide = turned[:, 0:128]
-        for start in range(128, queries, 128):
-            wide = jnp.maximum(wide, turned[:, start : start + 128])
+        keys = unpacked(got_ref, source // sources)
+        late = key_lateness(got_ref, source, sources)
+        wide = jnp.full((TILE, 128), -1.0, F32)
+        for number in range(queries // TILE):
+            columns = slice(number * TILE, (number + 1) * TILE)
+            scores = score(keys, rows_ref[columns, :])
+            later = late > query_late_ref[:, columns]
+            best[number] = jnp.maximum(best[number], fold(jnp.where(later, scores, -1.0)))
+            turned = jnp.where(later, -1.0, scores)
+            for start in range(0, TILE, 128):
+                wide = jnp.maximum(wide, turned[:, start : start + 128])
         found = jnp.max(wide, axis=1, keepdims=True)
-        found = jnp.broadcast_to(found, (TILE, 128)).reshape(sources, MOST, 128)
         shape = (sources, MOST, 128)
+        found = jnp.broadcast_to(found, (TILE, 128)).reshape(shape)
         placed = jnp.where(iota(shape, 1) == iota(shape, 2), found, 0.0)
         back_ref[other_at + source : other_at + source + sources] = jnp.sum(
             placed, axis=1
         ).reshape(sources, 1, 128)
-    if queries < HALF:
-        best = jnp.concatenate([best, best_ref[:, queries:HALF]], axis=1)
-    best = jnp.max(best, axis=0, keepdims=True)
+    best = jnp.max(jnp.concatenate(best, axis=1), axis=0, keepdims=True)
     back_ref[own_at : own_at + CHIPS] = by_source(best).reshape(CHIPS, 1, 128)
 
 
@@ -226,10 +232,10 @@
 def finish(back_ref, place_ref, out_ref):
     back = jnp.maximum(back_ref[0:CHIPS], back_ref[CHIPS : 2 * CHIPS]).reshape(CHIPS, 128)
     member = (iota((CHIPS, ROWS), 0) == place_ref[0:1, :]).astype(BF16)
-    columns = lax.dot_general(
-        jnp.concatenate(exact_parts(back), axis=0),
+    turned = jnp.transpose(back)[0:THIRD, :]
+    columns = jnp.dot(
+        jnp.concatenate(exact_parts(turned), axis=1),
         jnp.concatenate([member, member, member], axis=0),
-        (((0,), (0,)), ((), ())),
         preferred_element_type=F32,
     )
     here = iota((THIRD, ROWS), 0) == place_ref[1:2, :]

time: 80.6 us -> 80.6 us (level)
  no operation moved by 1% of the time
where the time goes in v8:
time: 80.6 us; the launch traced here: 80.4 us
  blocking collectives  65 us (81%)
  Pallas kernels  11.9 us (15%)
  starting transfers between devices  3.11 us (4%)
    all_to_all x1, blocking collectives, per_device(): lax.all_to_all(send, CHIP_AXES, split_axis=0, concat_axis=0, tiled=True)  52.2 us
    all_to_all x1, blocking collectives, per_device(): lax.all_to_all(back, BACK_AXES, split_axis=0, concat_axis=0, tiled=True)  12.9 us
    pallas_call x1, Pallas kernels, per_device(): pl.pallas_call(own_scores, out_shape=(shape((HALF, WIDTH), BF16), shape((...  5.12 us
    ppermute x1, starting transfers between devices, per_device(): other = lax.ppermute(got, 'c', [(0, 1), (1, 0)])  3.11 us
    pallas_call x1, Pallas kernels, per_device(): pl.pallas_call(other_scores, out_shape=shape((2 * CHIPS, 1, 128), F32), c...  3.1 us
    pallas_call x1, Pallas kernels, per_device(): pl.pallas_call(prepare, out_shape=(shape((CHIPS, CHUNK, 128), BF16), shap...  2.83 us
  transfers between devices with their start and end apart: 1, of which 1 were waited for; matrix products, arithmetic and copies ran while one was open for 0% of the time, Pallas kernels for 6%

profile of v8, /device:TPU:1, one launch (start us, length us, event | category | flops | bytes accessed | tf_op | source)
XLA Modules:
  0.0 80.4 jit_solution(10048308901620123209)
XLA Ops:
  0.0 2.8 %shard_map.37 = (bf16[64,200,128]{2,1,0:T(8,128)(2,1)S(1)}, s32[2,384]{1,0:T(2,128)S(1)}) custom-call(f32[384,1024]{1,0:T(8,128)} %emb_hbm.1, s32[1,384]{1,0:T(1,128)} %bitcast.1, s32[384]{0:T(512)} %order_hbm.1), custom_call_target="tpu_custom_call" | custom-call | tf_op jit(solution)/shard_map/pallas_call | solution.py:250
  2.8 52.2 %all_to_all.10.got_ref = bf16[64,200,128]{2,1,0:T(8,128)(2,1)S(1)} all-to-all(bf16[64,200,128]{2,1,0:T(8,128)(2,1)S(1)} %get-tuple-element.10), channel_id=1, replica_groups=mesh['x'=4,'y'=4,'z'=4,'c'=2] {'x','y','z'}, dimensions={0} | all-to-all | bytes 6553600 | tf_op jit(solution)/shard_map/all_to_all | solution.py:266
  55.0 3.1 %collective-permute-start = (bf16[64,200,128]{2,1,0:T(8,128)(2,1)S(1)}, bf16[64,200,128]{2,1,0:T(8,128)(2,1)S(1)}, u32[]{:S(2)}, u32[]{:S(2)}) collective-permute-start(bf16[64,200,128]{2,1,0:T(8,128)(2,1)S(1)} %all_to_all.10.got_ref), channel_id=1, source_target_pairs={{0,1},{1,0},{2,3},{3,2},{4,5},{5,4},{6,7},{7,6},{8,9},{9,8},{10,11... | collective-permute-start | bytes 9830408 | tf_op jit(solution)/shard_map/ppermute | solution.py:267
  58.1 5.1 %shard_map.38 = (bf16[1536,1024]{1,0:T(8,128)(2,1)S(1)}, f32[1,1536]{1,0:T(1,128)S(1)}, f32[8,1536]{1,0:T(8,128)S(1)}) custom-call(bf16[64,200,128]{2,1,0:T(8,128)(2,1)S(1)} %all_to_all.10.got_ref), custom_call_target="tpu_custom_call" | custom-call | flops 4831838208 | bytes 8388608 | tf_op jit(solution)/shard_map/pallas_call | solution.py:269
  63.2 0.3 collective-permute-done.got_ref
  63.6 3.1 %shard_map.39 = f32[128,1,128]{2,1,0:T(1,128)S(1)} custom-call(bf16[64,200,128]{2,1,0:T(8,128)(2,1)S(1)} %collective-permute-done.got_ref, bf16[1536,1024]{1,0:T(8,128)(2,1)S(1)} %get-tuple-element.11.rows_ref, f32[1,1536]{1,0:T(1,128)S(1)} %get-tuple-element.12.query_late_ref, f32[8,1536]{1,0:T(8,128)S(1)} %get-tuple-element.13.best_ref), custom_call_target="tpu_custom_call" | custom-call | flops 4831838208 | bytes 8388608 | tf_op jit(solution)/shard_map/pallas_call | solution.py:276
  66.7 12.9 %all_to_all.11.back_ref = f32[128,1,128]{2,1,0:T(1,128)S(1)} all-to-all(f32[128,1,128]{2,1,0:T(1,128)S(1)} %shard_map.39), channel_id=1, replica_groups=mesh['x'=4,'y'=4,'z'=4,'c'=2] {'c','x','y','z'}, dimensions={0} | all-to-all | bytes 131072 | tf_op jit(solution)/shard_map/all_to_all | solution.py:282
  79.6 0.9 %shard_map.40 = f32[384]{0:T(512)} custom-call(f32[128,1,128]{2,1,0:T(1,128)S(1)} %all_to_all.11.back_ref, s32[2,384]{1,0:T(2,128)S(1)} %get-tuple-element.14.place_ref), custom_call_target="tpu_custom_call" | custom-call | tf_op jit(solution)/shard_map/pallas_call | solution.py:283
Async XLA Ops:
  55.0 8.6 %collective-permute-start = (bf16[64,200,128]{2,1,0:T(8,128)(2,1)S(1)}, bf16[64,200,128]{2,1,0:T(8,128)(2,1)S(1)}, u32[]{:S(2)}, u32[]{:S(2)}) collective-permute-start(bf16[64,200,128]{2,1,0:T(8,128)(2,1)S(1)} %all_to_all.10.got_ref), channel_id=1, source_target_pairs={{0,1},{1,0},{2,3},{3,2},{4,5},{5,4},{6,7},{7,6},{8,9},{9,8},{10,11... | collective-permute-start | bytes 9830408 | tf_op jit(solution)/shard_map/ppermute | solution.py:267
